TPU v7x, 128 devices: a whole 4x4x4 slice. The times are simulated.
128 devices in a mesh: replica: 64 (over z, y, x), shard: 2 (over core).
Axes of the slice: x: 4, y: 4, z: 4, core: 2. Of those that a mesh axis runs over, the one named last changes fastest.
Arguments:
- tokens: bfloat16 [49152, 960], P(('replica', 'shard')), may hold values from -6 to 6
- starts: int32 [49152], P(('replica', 'shard')), may hold values from 0 to 383, as said below
- out_grad: bfloat16 [49152, 960], P(('replica', 'shard')), may hold values from -6 to 6
- norm_attn: bfloat16 [960], P('shard'), may hold values from 0.5 to 1.5
- norm_mlp: bfloat16 [960], P('shard'), may hold values from 0.5 to 1.5
- qkv_weight: bfloat16 [960, 1600], P('shard'), may hold values from -0.1875 to 0.1875
- out_weight: bfloat16 [960, 960], P('shard'), may hold values from -0.5 to 0.5
- gate_up_weight: bfloat16 [960, 5120], P('shard'), may hold values from -0.1875 to 0.1875
- down_weight: bfloat16 [2560, 960], P('shard'), may hold values from -0.25 to 0.25
Outputs:
- mixed: bfloat16 [49152, 960], P(('replica', 'shard'))
- input_grad: float32 [49152, 960], P(('replica', 'shard'))
- grad_norm_attn: float32 [960], P('shard')
- grad_norm_mlp: float32 [960], P('shard')
- grad_qkv: float32 [960, 1600], P('shard')
- grad_out: float32 [960, 960], P('shard')
- grad_gate_up: float32 [960, 5120], P('shard')
- grad_down: float32 [2560, 960], P('shard')
Inputs may be any that keep to these rules, and one draw needn't show every extreme that they name: starts[r] is the first row, counted within the 384 rows of r's device, of the sequence that holds r; sequences are whole on a device; the first device holds one sequence of 384 rows and the last row of all is a sequence of its own.
All inputs are finite; a program needn't handle non-finite values.
Results may differ from a plain program's by a relative error of at most 0.02.
Values may be sent and summed in bfloat16 or wider, within the bound.
A program may use at most 192 MiB of HBM per device.

v0:
```python
import math

import jax
import jax.numpy as jnp
from jax import lax
from jax.sharding import PartitionSpec as P

QUERY_HEADS = 15
KEY_VALUE_HEADS = 5
HEAD_SIZE = 64
FF = 2560


EPSILON = 1e-05


def in_one_piece(arrays, axis, dim, along):
    widths = [math.prod(a.shape[along:]) for a in arrays]
    both = jnp.concatenate(
        [a.reshape(*a.shape[:along], w) for a, w in zip(arrays, widths)], axis=along
    )
    filled = lax.all_gather(both, axis, axis=dim, tiled=True)
    parts = jnp.split(filled, [sum(widths[:k]) for k in range(1, len(widths))], axis=along)
    return tuple(
        (b.reshape(*filled.shape[:along], *a.shape[along:]) for a, b in zip(arrays, parts))
    )


def sent_together(arrays, axis, dim, along):
    columns = [a.reshape(*a.shape[:along], -1) for a in arrays]
    both = jnp.concatenate(columns, axis=along)
    filled, at, finished = (lax.psum_scatter(both, axis, scatter_dimension=dim, tiled=True), 0, [])
    for a, column in zip(arrays, columns):
        piece = filled[..., at : at + column.shape[along]]
        finished.append(piece.reshape(*piece.shape[:along], *a.shape[along:]))
        at += column.shape[along]
    return tuple(finished)


def in_blocks(shard, dim, length):
    shape = shard.shape
    parts = shard.reshape(*shape[:dim], length, shape[dim] // length, *shape[dim + 1 :])
    return jnp.moveaxis(parts, dim, 0)


def sum_together(arrays, axis, dims):
    length = lax.axis_size(axis)
    parts = [in_blocks(a, dim, length) for a, dim in zip(arrays, dims)]
    lines = jnp.concatenate([b.reshape(length, -1) for b in parts], axis=1)
    extent = max(16, -(-lines.shape[1] // 1024) * 8)
    lines = jnp.pad(lines, ((0, 0), (0, extent * 128 - lines.shape[1]))).reshape(-1, 128)
    line, at, finished = (lax.psum_scatter(lines, axis, tiled=True).reshape(-1), 0, [])
    for b in parts:
        part = b[0]
        finished.append(line[at : at + part.size].reshape(part.shape))
        at += part.size
    return tuple(finished)


def sent_together_2(arrays, axis, dim, along):
    ends, at = ([], 0)
    for a in arrays[:-1]:
        at += a.shape[along]
        ends.append(at)
    both = jnp.concatenate(arrays, axis=along)
    return tuple(jnp.split(lax.all_gather(both, axis, axis=dim, tiled=True), ends, axis=along))


def norm_rows(values, gain):
    scale_inv = lax.rsqrt(jnp.mean(values * values, axis=-1, keepdims=True) + EPSILON)
    normed = values * scale_inv
    return (normed, scale_inv, normed * gain)


def norm_back(grad_scaled, normed, scale_inv, gain):
    grad_gain = jnp.sum(grad_scaled * normed, axis=0)
    grad_normed = grad_scaled * gain
    grad_in = scale_inv * (
        grad_normed - normed * jnp.mean(grad_normed * normed, axis=-1, keepdims=True)
    )
    return (grad_in, grad_gain)


def rope_tables(starts):
    token_rows = jnp.arange(starts.shape[0], dtype=jnp.int32)
    position = (token_rows - starts).astype(jnp.float32)
    half = HEAD_SIZE // 2
    freq = jnp.exp(
        -jnp.log(jnp.float32(10000.0)) * jnp.arange(half, dtype=jnp.float32) * 2.0 / HEAD_SIZE
    )
    angle = position[:, None] * freq[None, :]
    return (jnp.cos(angle)[:, None, :], jnp.sin(angle)[:, None, :])


def rotate_halves(values, cosine_table, sine_table):
    half = HEAD_SIZE // 2
    first = values[..., :half]
    second = values[..., half:]
    return jnp.concatenate(
        [first * cosine_table - second * sine_table, second * cosine_table + first * sine_table],
        axis=-1,
    )


def rotate_back(grads, cosine_table, sine_table):
    half = HEAD_SIZE // 2
    first = grads[..., :half]
    second = grads[..., half:]
    return jnp.concatenate(
        [first * cosine_table + second * sine_table, second * cosine_table - first * sine_table],
        axis=-1,
    )


def transpose_dot(left, right):
    return jnp.einsum("ta,tb->ab", left, right, preferred_element_type=jnp.float32)


def split_ready(piece, replicas):
    if piece.ndim == 2 and piece.shape[1] % replicas == 0:
        return piece
    flat = piece.reshape(1, piece.size)
    padding = -piece.size % replicas
    return jnp.pad(flat, ((0, 0), (0, padding)))


def split_undo(summed, piece):
    if summed.shape == piece.shape:
        return summed
    return summed.reshape(summed.size)[: piece.size]


def per_device(
    tokens,
    starts,
    out_grad,
    norm_attn,
    norm_mlp,
    qkv_weight,
    out_weight,
    gate_up_weight,
    down_weight,
):
    token_rows = tokens.shape[0]
    group_factor = QUERY_HEADS // KEY_VALUE_HEADS
    scale = HEAD_SIZE ** (-0.5)
    replicas = lax.axis_size("replica")
    owned = (norm_attn, norm_mlp, qkv_weight, out_weight, gate_up_weight, down_weight)
    gathered = (
        lax.all_gather(owned[0], "shard", axis=0, tiled=True),
        *in_one_piece((owned[1], owned[2], owned[3], owned[4]), "shard", 0, 1),
        lax.all_gather(owned[5], "shard", axis=0, tiled=True),
    )
    gain_one = gathered[0].astype(jnp.float32)
    gain_two = gathered[1].astype(jnp.float32)
    w_qkv, w_out, w_gu, w_down = (gathered[2], gathered[3], gathered[4], gathered[5])
    values = tokens.astype(jnp.float32)
    normed_one, inv_one, scaled_one = norm_rows(values, gain_one)
    hidden_one = scaled_one.astype(jnp.bfloat16)
    joint_projection = jnp.dot(hidden_one, w_qkv, preferred_element_type=jnp.float32)
    cosine_table, sine_table = rope_tables(starts)
    query_rows = rotate_halves(
        joint_projection[:, : QUERY_HEADS * HEAD_SIZE].reshape(token_rows, QUERY_HEADS, HEAD_SIZE),
        cosine_table,
        sine_table,
    ).astype(jnp.bfloat16)
    key_rot = rotate_halves(
        joint_projection[
            :, QUERY_HEADS * HEAD_SIZE : (QUERY_HEADS + KEY_VALUE_HEADS) * HEAD_SIZE
        ].reshape(token_rows, KEY_VALUE_HEADS, HEAD_SIZE),
        cosine_table,
        sine_table,
    ).astype(jnp.bfloat16)
    value_rows = (
        joint_projection[:, (QUERY_HEADS + KEY_VALUE_HEADS) * HEAD_SIZE :]
        .reshape(token_rows, KEY_VALUE_HEADS, HEAD_SIZE)
        .astype(jnp.bfloat16)
    )
    grouped_query = query_rows.reshape(token_rows, KEY_VALUE_HEADS, group_factor, HEAD_SIZE)
    scores = (
        jnp.einsum("qhgd,khd->hgqk", grouped_query, key_rot, preferred_element_type=jnp.float32)
        * scale
    )
    index = jnp.arange(token_rows, dtype=jnp.int32)
    seen = (starts[:, None] == starts[None, :]) & (index[:, None] >= index[None, :])
    scores = jnp.where(seen[None, None], scores, -1e30)
    peak = jnp.max(scores, axis=-1, keepdims=True)
    expo = jnp.exp(scores - peak)
    probs = expo / jnp.sum(expo, axis=-1, keepdims=True)
    probs_low = probs.astype(jnp.bfloat16)
    attended = jnp.einsum(
        "hgqk,khd->qhgd", probs_low, value_rows, preferred_element_type=jnp.float32
    )
    attended = attended.reshape(token_rows, QUERY_HEADS * HEAD_SIZE).astype(jnp.bfloat16)
    mid = values + jnp.dot(attended, w_out, preferred_element_type=jnp.float32)
    normed_two, inv_two, scaled_two = norm_rows(mid, gain_two)
    hidden_two = scaled_two.astype(jnp.bfloat16)
    gate_up = jnp.dot(hidden_two, w_gu, preferred_element_type=jnp.float32)
    gate = gate_up[:, :FF]
    upper = gate_up[:, FF:]
    sigma = jax.nn.sigmoid(gate)
    inner = (gate * sigma * upper).astype(jnp.bfloat16)
    result = mid + jnp.dot(inner, w_down, preferred_element_type=jnp.float32)
    mixed = result.astype(jnp.bfloat16)
    back_one, back_two = (gain_one, gain_two)
    b_qkv, b_out, b_gu, b_down = (w_qkv, w_out, w_gu, w_down)
    grad_down = transpose_dot(inner, out_grad)
    grad_inner = jnp.dot(out_grad, b_down.T, preferred_element_type=jnp.float32)
    grad_upper = grad_inner * gate * sigma
    grad_gate = grad_inner * upper * sigma * (1.0 + gate * (1.0 - sigma))
    grad_gu = jnp.concatenate([grad_gate, grad_upper], axis=1).astype(jnp.bfloat16)
    grad_gate_up = transpose_dot(hidden_two, grad_gu)
    grad_hidden_two = jnp.dot(grad_gu, b_gu.T, preferred_element_type=jnp.float32)
    grad_mid_norm, grad_gain_two = norm_back(grad_hidden_two, normed_two, inv_two, back_two)
    grad_mid = out_grad.astype(jnp.float32) + grad_mid_norm
    grad_attn = grad_mid.astype(jnp.bfloat16)
    grad_out = transpose_dot(attended, grad_attn)
    attended_gradient = jnp.dot(grad_attn, b_out.T, preferred_element_type=jnp.float32).astype(
        jnp.bfloat16
    )
    grouped_gradient = attended_gradient.reshape(
        token_rows, KEY_VALUE_HEADS, group_factor, HEAD_SIZE
    )
    grad_probs = jnp.einsum(
        "qhgd,khd->hgqk", grouped_gradient, value_rows, preferred_element_type=jnp.float32
    )
    value_gradient = jnp.einsum(
        "hgqk,qhgd->khd", probs_low, grouped_gradient, preferred_element_type=jnp.float32
    )
    delta = jnp.sum(grad_probs * probs, axis=-1, keepdims=True)
    grad_scores = (probs * (grad_probs - delta)).astype(jnp.bfloat16)
    grad_query = (
        jnp.einsum("hgqk,khd->qhgd", grad_scores, key_rot, preferred_element_type=jnp.float32)
        * scale
    )
    key_gradient = (
        jnp.einsum("hgqk,qhgd->khd", grad_scores, grouped_query, preferred_element_type=jnp.float32)
        * scale
    )
    grad_query = rotate_back(
        grad_query.reshape(token_rows, QUERY_HEADS, HEAD_SIZE), cosine_table, sine_table
    )
    key_gradient = rotate_back(key_gradient, cosine_table, sine_table)
    grad_joint = jnp.concatenate(
        [
            grad_query.reshape(token_rows, QUERY_HEADS * HEAD_SIZE),
            key_gradient.reshape(token_rows, KEY_VALUE_HEADS * HEAD_SIZE),
            value_gradient.reshape(token_rows, KEY_VALUE_HEADS * HEAD_SIZE),
        ],
        axis=1,
    ).astype(jnp.bfloat16)
    grad_qkv = transpose_dot(hidden_one, grad_joint)
    grad_hidden_one = jnp.dot(grad_joint, b_qkv.T, preferred_element_type=jnp.float32)
    grad_in_norm, grad_gain_one = norm_back(grad_hidden_one, normed_one, inv_one, back_one)
    input_grad = grad_mid + grad_in_norm
    owner = (
        lax.psum_scatter(
            grad_gain_one.astype(jnp.bfloat16), "shard", scatter_dimension=0, tiled=True
        ).astype(jnp.float32),
        *tuple(
            (
                part.astype(jnp.float32)
                for part in sent_together(
                    (
                        grad_gain_two.astype(jnp.bfloat16),
                        grad_qkv.astype(jnp.bfloat16),
                        grad_out.astype(jnp.bfloat16),
                        grad_gate_up.astype(jnp.bfloat16),
                    ),
                    "shard",
                    0,
                    1,
                )
            )
        ),
        lax.psum_scatter(
            grad_down.astype(jnp.bfloat16), "shard", scatter_dimension=0, tiled=True
        ).astype(jnp.float32),
    )
    ready = [split_ready(piece, replicas) for piece in owner]
    reduced = sum_together(
        (ready[0], ready[1], ready[2], ready[3], ready[4], ready[5]), "replica", (1, 1, 1, 1, 1, 1)
    )
    spread = (
        *tuple(
            (
                part.astype(jnp.float32)
                for part in sent_together_2(
                    (reduced[0].astype(jnp.bfloat16), reduced[1].astype(jnp.bfloat16)),
                    "replica",
                    1,
                    0,
                )
            )
        ),
        lax.all_gather(reduced[2].astype(jnp.bfloat16), "replica", axis=1, tiled=True).astype(
            jnp.float32
        ),
        lax.all_gather(reduced[3].astype(jnp.bfloat16), "replica", axis=1, tiled=True).astype(
            jnp.float32
        ),
        lax.all_gather(reduced[4].astype(jnp.bfloat16), "replica", axis=1, tiled=True).astype(
            jnp.float32
        ),
        lax.all_gather(reduced[5].astype(jnp.bfloat16), "replica", axis=1, tiled=True).astype(
            jnp.float32
        ),
    )
    outputs = [split_undo(spread[number], owner[number]) for number in range(6)]
    return (
        mixed,
        input_grad,
        outputs[0],
        outputs[1],
        outputs[2],
        outputs[3],
        outputs[4],
        outputs[5],
    )


def solution(mesh):
    return jax.shard_map(
        per_device,
        mesh=mesh,
        in_specs=(
            P(("replica", "shard"), None),
            P(("replica", "shard")),
            P(("replica", "shard"), None),
            P("shard"),
            P("shard"),
            P("shard", None),
            P("shard", None),
            P("shard", None),
            P("shard", None),
        ),
        out_specs=(
            P(("replica", "shard"), None),
            P(("replica", "shard"), None),
            P("shard"),
            P("shard"),
            P("shard", None),
            P("shard", None),
            P("shard", None),
            P("shard", None),
        ),
        check_vma=False,
    )
```

profile of v0, /device:TPU:0, one launch (start us, length us, event | category | flops | bytes accessed | tf_op | source)
XLA Modules:
  0.0 1196.9 jit_solution(17813849681442280290)
XLA Ops:
  8.0 13.7 %concatenate.42 = bf16[480,7681]{1,0:T(8,128)(2,1)} concatenate(bf16[480,1]{1,0:T(8,128)(2,1)S(1)} %reshape.310, bf16[480,1600]{1,0:T(8,128)(2,1)} %param.14, bf16[480,960]{1,0:T(8,128)(2,1)} %param.15, bf16[480,5120]{1,0:T(8,128)(2,1)} %param.16), dimensions={1} | concatenate | bytes 14747520 | tf_op jit(solution)/shard_map/concatenate | solution.py:19
  27.3 27.2 %all-gather.10.cloned.1.call-done = bf16[960,7681]{1,0:T(8,128)(2,1)} async-done(((bf16[480,7681]{1,0:T(8,128)(2,1)}), bf16[960,7681]{1,0:T(8,128)(2,1)}) %all-gather.10.cloned.1.call-update) | async-done | bytes 14747536 | tf_op jit(solution)/shard_map/all_gather | solution.py:22
  61.4 6.8 fusion.72
  68.2 5.8 fusion.40
  78.1 12.3 %fusion.6 = f32[384,5120]{1,0:T(8,128)} fusion(bf16[960,7681]{1,0:T(8,128)(2,1)} %all-gather.10.cloned.1.call-done, f32[384,960]{0,1:T(8,128)S(1)} %get-tuple-element.50, f32[960]{0:T(1024)S(1)} %convert_reduce_fusion, f32[384]{0:T(512)S(1)} %add_rsqrt_fusion), kind=kOutput, calls=%fused_computation.12 | convolution fusion | flops 3775979520 | bytes 19174656 | tf_op jit(solution)/shard_map/dot_general | solution.py:198
  90.5 10.6 multiply_convert_fusion.1
  107.2 10.6 multiply_reduce_fusion
  122.6 9.3 fusion.1
  131.9 9.8 fusion.3
  156.4 7.9 convolution_convert_fusion
  164.3 26.0 %concatenate.51 = bf16[960,7681]{1,0:T(8,128)(2,1)} concatenate(bf16[960,1]{1,0:T(8,128)(2,1)S(1)} %copy-done.4, bf16[960,1600]{1,0:T(8,128)(2,1)} %convolution_convert_fusion.2, bf16[960,960]{1,0:T(8,128)(2,1)} %convolution_convert_fusion.3, bf16[960,5120]{1,0:T(8,128)(2,1)} %convolution_convert_fusion), dimensions={1} | concatenate | bytes 29495040 | tf_op jit(solution)/shard_map/concatenate | solution.py:31
  191.3 5.5 fusion.33
  205.7 9.9 copy.55
  215.6 8.5 reshape.280
  224.1 5.9 copy.58
  241.9 7.3 copy.75
  249.2 11.0 reshape.311
  277.9 6.7 slice.143
  284.6 7.8 copy.53
  292.4 9.7 copy.54
  302.1 17.2 %reshape.278 = bf16[64,38400]{1,0:T(8,128)(2,1)} reshape(bf16[64,480,80]{2,1,0:T(8,128)(2,1)} %copy.54) | data formatting | bytes 9830400 | tf_op jit(solution)/shard_map/reshape | solution.py:49
  320.9 11.6 dynamic-update-slice.3
  332.5 7.4 dynamic-update-slice.4
  339.9 27.6 %dynamic-update-slice.5 = bf16[64,76816]{1,0:T(8,128)(2,1)} dynamic-update-slice(bf16[64,76816]{1,0:T(8,128)(2,1)} %dynamic-update-slice.4, bf16[64,38400]{1,0:T(8,128)(2,1)} %reshape.278, s32[]{} %constant.52, s32[]{} %constant.56) | dynamic-update-slice | bytes 9830404
  367.5 16.3 %dynamic-update-slice.6 = bf16[64,76816]{1,0:T(8,128)(2,1)} dynamic-update-slice(bf16[64,76816]{1,0:T(8,128)(2,1)} %dynamic-update-slice.5, bf16[64,19200]{1,0:T(8,128)(2,1)} %copy.58, s32[]{} %constant.52, s32[]{} %constant.57) | dynamic-update-slice | bytes 4915204 | tf_op jit(solution)/shard_map/concatenate | solution.py:49
  383.8 11.8 pad_convert_fusion
  395.6 16.1 %reshape.286 = f32[38912,128]{1,0:T(8,128)} reshape(f32[64,77824]{1,0:T(8,128)} %pad_convert_fusion) | data formatting | bytes 39845888 | tf_op jit(solution)/shard_map/reshape | solution.py:51
  411.8 394.9 %reduce-scatter.8.cloned.1.call-done = f32[608,128]{1,0:T(8,128)} async-done(((f32[38912,128]{1,0:T(8,128)}), f32[608,128]{1,0:T(8,128)}) %reduce-scatter.8.cloned.1.call-update) | async-done | bytes 311312 | tf_op jit(solution)/shard_map/reduce_scatter | solution.py:52
  814.7 6.0 add_convert_fusion
  820.9 171.3 %all-gather = bf16[64,8,2]{1,2,0:T(2,128)(2,1)S(1)} all-gather(bf16[1,8,2]{1,2,0:T(2,128)(2,1)S(1)} %maximum_bitcast_fusion.6), channel_id=1, replica_groups=mesh['replica'=64,'shard'=2] {'replica'}, dimensions={0}, use_global_device_ids=true | all-gather | bytes 2080 | tf_op jit(solution)/shard_map/all_gather | solution.py:66
  992.7 175.8 %all-gather.2 = bf16[64,15,480]{2,1,0:T(8,128)(2,1)S(1)} all-gather(bf16[1,15,480]{2,1,0:T(8,128)(2,1)S(1)} %bitcast.153), channel_id=1, replica_groups=mesh['replica'=64,'shard'=2] {'replica'}, dimensions={0}, use_global_device_ids=true | all-gather | bytes 936000 | tf_op jit(solution)/shard_map/all_gather | solution.py:299
  1181.6 8.1 copy.66
  (167 shorter events, 103.6 us)
Async XLA Ops:
  7.2 47.4 %all-gather.10.cloned.1.call-start = ((), (), s32[]{:S(2)}) async-start(), calls=%async_computation.3 | async-start | bytes 22487040 | tf_op jit(solution)/shard_map/all_gather | solution.py:22
  21.8 4.8 copy-start.1
  21.8 5.0 copy-start.19
  21.8 68.6 %all-gather.12.cloned.1.call-start = ((), (), s32[]{:S(2)}) async-start(), calls=%async_computation.4 | async-start | bytes 7372800 | tf_op jit(solution)/shard_map/all_gather | solution.py:152
  22.6 178.6 %reduce-scatter.6.cloned.1.call-start = ((), (), s32[]{:S(2)}) async-start(), calls=%async_computation.6 | async-start | bytes 7372800 | tf_op jit(solution)/shard_map/reduce_scatter | solution.py:276
  59.8 8.4 copy-start.12
  61.2 7.0 copy-start.10
  61.4 6.8 copy-start.3
  68.2 5.9 copy-start.16
  74.1 4.1 copy-start.7
  78.1 12.4 %copy-start.5 = (bf16[384,960]{0,1:T(8,128)(2,1)S(1)}, bf16[384,960]{0,1:T(8,128)(2,1)}, u32[]{:S(2)}) copy-start(bf16[384,960]{0,1:T(8,128)(2,1)} %param.11) | copy-start | bytes 2211844
  106.7 123.4 %reduce-scatter.4.cloned.1.call-start = ((), (), s32[]{:S(2)}) async-start(), calls=%async_computation.5 | async-start | bytes 22487040 | tf_op jit(solution)/shard_map/reduce_scatter | solution.py:32
  107.2 11.5 copy-start.6
  119.1 3.6 copy-start.13
  119.1 3.6 copy-start.17
  122.6 9.3 copy-start.22
  141.7 4.1 copy-start
  141.7 4.1 copy-start.11
  145.9 6.9 copy-start.14
  145.9 5.3 slice-start
  145.9 5.2 slice-start.1
  146.9 4.3 slice-start.2
  148.5 4.3 copy-start.9
  148.5 2.7 copy-start.23
  152.8 3.7 copy-start.26
  152.8 3.7 copy-start.27
  156.4 7.9 copy-start.4
  190.3 616.3 %reduce-scatter.8.cloned.1.call-start = ((), (), s32[]{:S(2)}) async-start(), calls=%async_computation.7 | async-start | bytes 20234240 | tf_op jit(solution)/shard_map/reduce_scatter | solution.py:52
  411.7 759.6 %all-gather.16.cloned.1.call-start = ((), (), s32[]{:S(2)}) async-start(), calls=%async_computation.9 | async-start | bytes 2129920 | tf_op jit(solution)/shard_map/all_gather | solution.py:296
  808.8 368.1 %all-gather.18.cloned.1.call-start = ((), (), s32[]{:S(2)}) async-start(), calls=%async_computation.10 | async-start | bytes 2662400 | tf_op jit(solution)/shard_map/all_gather | solution.py:305
  810.3 371.2 %all-gather.14.cloned.1.call-start = ((), (), s32[]{:S(2)}) async-start(), calls=%async_computation.8 | async-start | bytes 5324800 | tf_op jit(solution)/shard_map/all_gather | solution.py:302
  811.5 3.2 copy-start.25
  (7 other events, 11.1 us)
Sparse Core Ops, SparseCore 0:
  21.9 32.5 all-gather.9
  56.2 18.7 all-gather.11
  106.8 16.8 reduce-scatter.5
  190.5 28.3 reduce-scatter.3
  411.8 394.8 reduce-scatter.7
  810.4 61.8 all-gather.15
  876.1 64.0 all-gather.17
  944.0 68.2 all-gather.13
where the time goes:
time: 1210 us; the launch traced here: 1200 us
  waiting for transfers between devices  423 us (35%)
  blocking collectives  352 us (29%)
  local copies, waits for them, and re-layouts  270 us (22%)
  matrix products  105 us (9%)
  other arithmetic  29.2 us (2%)
  between operations  16.5 us (1%)
    reduce_scatter x1, waiting for transfers between devices, sum_together(): lax.psum_scatter(lines, axis, tiled=True).reshape(-1)  395 us
    all_gather x1, blocking collectives, per_device(): lax.all_gather(reduced[3].astype(jnp.bfloat16), 'replica', axis=1, tiled=...  176 us
    all_gather x1, blocking collectives, sent_together_2(): lax.all_gather(both, axis, axis=dim, tiled=True)  171 us
    unnamed x78, local copies, waits for them, and re-layouts  67.9 us
    reshape x7, local copies, waits for them, and re-layouts, sum_together(): lines = jnp.concatenate([b.reshape(length, -1) for b in parts], axis=1)  56.6 us
    all_gather x1, waiting for transfers between devices, in_one_piece(): filled = lax.all_gather(both, axis, axis=dim, tiled=True)  27.2 us
    slice x7, local copies, waits for them, and re-layouts, sent_together(): piece = filled[..., at:at + column.shape[along]]  27.2 us
    concatenate x1, local copies, waits for them, and re-layouts, sent_together(): both = jnp.concatenate(columns, axis=along)  26 us
  transfers between devices with their start and end apart: 8, of which 2 were waited for; matrix products, arithmetic and copies ran while one was open for 15% of the time, Pallas kernels for 0%

commit v1 on v0

v1 whole, which is shorter than its diff:
```python
import functools

import jax
import jax.numpy as jnp
from jax import lax
from jax.experimental import pallas as pl
from jax.experimental.pallas import tpu as pltpu
from jax.sharding import PartitionSpec as P

D = 960
HALF = D // 2
QUERY_HEADS = 15
KEY_VALUE_HEADS = 5
GROUP = QUERY_HEADS // KEY_VALUE_HEADS
HEAD_SIZE = 64
FF = 2560
TOK = 384
QKV = 1600
EPSILON = 1e-05
SCALE = HEAD_SIZE**-0.5
HIDDEN = -1e30

MESH = pl.DeviceIdType.MESH
F32 = jnp.float32
BF16 = jnp.bfloat16
LANES = 128
ROWS = 16
BLOCK = 48

FF_CHUNKS = 5
FF_TILES = 384
FF_USED = 360
OUT_BASE = FF_CHUNKS * FF_TILES
OUT_TILES = 256
OUT_USED = 225
QKV_BASE = OUT_BASE + OUT_TILES
QKV_TILES = 384
QKV_USED = 375
GAIN_TILE = 375
TILES = QKV_BASE + QKV_TILES
BOX = 376
UNITS = (2, 2, 2)
OUT_UNITS = (2, 2)
FF_EXTRA = 378
OUT_EXTRA_BASE = FF_CHUNKS * FF_EXTRA
QKV_EXTRA_BASE = OUT_EXTRA_BASE + 252
EXTRA = QKV_EXTRA_BASE + FF_EXTRA
STEPS = 13

OUT_TICK = 2 * FF_CHUNKS
ATTN_TICK = OUT_TICK + 1
LAST_TICK = ATTN_TICK + KEY_VALUE_HEADS
TICKS = LAST_TICK + 1 + STEPS


def mm(a, b):
    return lax.dot_general(a, b, (((1,), (0,)), ((), ())), preferred_element_type=F32)


def mm_nt(a, b):
    return lax.dot_general(a, b, (((1,), (1,)), ((), ())), preferred_element_type=F32)


def neighbours():
    r = lax.axis_index("replica")
    x = lax.rem(r, 4)
    y = lax.rem(lax.div(r, 4), 4)
    z = lax.div(r, 16)
    out = []
    for place, stride in ((x, 1), (y, 4), (z, 16)):
        ahead = r + stride * (lax.rem(place + 1, 4) - place)
        behind = r + stride * (lax.rem(place + 3, 4) - place)
        out.append((place, ahead, behind))
    return out


def add_into(dst, at, terms, count):
    block = 8 if count % 8 == 0 else count

    def step(i, _):
        o = i * block
        total = dst[pl.ds(at + o, block)].astype(F32)
        for ref, off in terms:
            total = total + ref[pl.ds(off + o, block)].astype(F32)
        dst[pl.ds(at + o, block)] = total.astype(BF16)
        return 0

    if count == block:
        step(0, 0)
    else:
        lax.fori_loop(0, count // block, step, 0)


class Travel:
    def __init__(self, work, extra, result, sems, group, base, extra_base, units):
        self.work, self.extra, self.result, self.group = work, extra, result, group
        self.send, self.recv, self.back_send, self.back_recv, self.keep_sem = sems
        core = lax.axis_index("shard")
        near = neighbours()
        self.there, self.back, self.keeps = [[], [], []], [[], [], []], []
        for color, n in enumerate(units):
            seg = base + 64 * n * color
            at = extra_base + 63 * n * color
            for phase in range(3):
                place, ahead, behind = near[(color + phase) % 3]
                chunk = (16, 4, 1)[phase] * n
                first = chunk // 2
                second = chunk - first
                mine = seg + chunk * place
                plus = seg + chunk * lax.rem(place + 1, 4)
                minus = seg + chunk * lax.rem(place + 3, 4)
                far = seg + chunk * lax.rem(place + 2, 4)
                xa, xb, yp, ym = at, at + first, at + chunk, at + 2 * chunk
                at = at + 3 * chunk

                def out(k, src, count, dst, to, color=color, phase=phase):
                    index = color * 18 + phase * 6 + k
                    return pltpu.make_async_remote_copy(
                        src_ref=work.at[pl.ds(src, count)],
                        dst_ref=extra.at[pl.ds(dst, count)],
                        send_sem=self.send.at[group, index],
                        recv_sem=self.recv.at[group, index],
                        device_id=(to, core),
                        device_id_type=MESH,
                    )

                def home(k, source, at, count, to, color=color, phase=phase):
                    index = color * 12 + phase * 4 + k
                    return pltpu.make_async_remote_copy(
                        src_ref=source.at[pl.ds(at, count)],
                        dst_ref=result.at[pl.ds(at, count)],
                        send_sem=self.back_send.at[group, index],
                        recv_sem=self.back_recv.at[group, index],
                        device_id=(to, core),
                        device_id_type=MESH,
                    )

                self.there[phase].append((
                    (
                        lambda out=out, far=far, first=first, xa=xa, to=ahead: out(0, far, first, xa, to),
                        lambda out=out, far=far, first=first, second=second, xb=xb, to=behind: out(1, far + first, second, xb, to),
                        lambda out=out, plus=plus, first=first, second=second, yp=yp, to=ahead: out(2, plus + first, second, yp + first, to),
                        lambda out=out, minus=minus, first=first, ym=ym, to=behind: out(3, minus, first, ym, to),
                        lambda out=out, plus=plus, first=first, yp=yp, to=ahead: out(4, plus, first, yp, to),
                        lambda out=out, minus=minus, first=first, second=second, ym=ym, to=behind: out(5, minus + first, second, ym + first, to),
                    ),
                    (first, second, chunk, xa, xb, yp, ym, mine, plus, minus),
                ))
                source = work if phase == 2 else result
                self.back[phase].append((
                    lambda home=home, source=source, mine=mine, chunk=chunk, to=ahead: home(0, source, mine, chunk, to),
                    lambda home=home, source=source, mine=mine, chunk=chunk, to=behind: home(1, source, mine, chunk, to),
                    lambda home=home, minus=minus, first=first, to=ahead: home(2, result, minus, first, to),
                    lambda home=home, plus=plus, first=first, second=second, to=behind: home(3, result, plus + first, second, to),
                ))
                if phase == 2:
                    self.keeps.append(
                        lambda mine=mine, chunk=chunk, color=color: pltpu.make_async_copy(
                            work.at[pl.ds(mine, chunk)],
                            result.at[pl.ds(mine, chunk)],
                            self.keep_sem.at[group, color],
                        )
                    )
                seg = mine

    def step(self, k):
        if k < 6 and k % 2 == 1:
            for c, (first, second, chunk, xa, xb, yp, ym, mine, plus, minus) in self.there[k // 2]:
                c[0]().wait_recv()
                add_into(self.work, plus, [(self.extra, xa)], first)
                c[4]().start()
                c[1]().wait_recv()
                add_into(self.work, minus + first, [(self.extra, xb)], second)
                c[5]().start()
            return
        if k in (2, 4, 6):
            for c, (first, second, chunk, xa, xb, yp, ym, mine, plus, minus) in self.there[k // 2 - 1]:
                for i in (2, 3, 4, 5):
                    c[i]().wait_recv()
                add_into(self.work, mine, [(self.extra, yp), (self.extra, ym)], chunk)
        if k in (0, 2, 4):
            for c, _ in self.there[k // 2]:
                for i in (0, 1, 2, 3):
                    c[i]().start()
        if k in (7, 9, 11):
            phase = (11 - k) // 2
            for n, c in enumerate(self.back[phase]):
                c[0]().wait_recv()
                c[2]().start()
                c[1]().wait_recv()
                c[3]().start()
                if phase == 2:
                    self.keeps[n]().wait()
        if k in (8, 10, 12):
            for c in self.back[(12 - k) // 2]:
                c[2]().wait_recv()
                c[3]().wait_recv()
        if k in (6, 8, 10):
            phase = (10 - k) // 2
            for n, c in enumerate(self.back[phase]):
                c[0]().start()
                c[1]().start()
                if phase == 2:
                    self.keeps[n]().start()

    def finish(self):
        for phase in range(3):
            for c, _ in self.there[phase]:
                for i in range(6):
                    c[i]().wait_send()
            for c in self.back[phase]:
                for i in range(4):
                    c[i]().wait_send()


def layer_kernel(
    tokens, starts, out_grad, gains, qkv_w, out_w, gu_w, down_w,
    mixed, input_grad, result, gu_far, down_far,
    tok, dyt, dyp, gain_far, wqkv, wout, wg, wd,
    cosine, sine, bias, hbuf, h1t, h2t, qs, ks, vs, ps, os, qt, dot_, ot,
    x1, yacc, dh2, kvt, dqkv, gacc1, gacc2, gain_sum, box, work, extra,
    in_sem, own_sem, load_sem, w_send, w_recv, pair_send, pair_recv, out_sem,
    send, recv, back_send, back_recv, keep_sem,
):
    r = lax.axis_index("replica")
    core = lax.axis_index("shard")
    other = 1 - core
    sems = (send, recv, back_send, back_recv, keep_sem)

    copy_tok = pltpu.make_async_copy(tokens, h2t, in_sem.at[0])
    copy_dy = pltpu.make_async_copy(out_grad, dyt, in_sem.at[1])
    copy_tok.start()
    copy_dy.start()
    mine480 = pl.ds(pl.multiple_of(core * HALF, 16), HALF)
    other480 = pl.ds(pl.multiple_of(other * HALF, 16), HALF)
    own_qkv = pltpu.make_async_copy(qkv_w, wqkv.at[mine480], own_sem.at[0])
    own_out = pltpu.make_async_copy(out_w, wout.at[mine480], own_sem.at[1])
    own_qkv.start()
    own_out.start()

    barrier = pltpu.get_barrier_semaphore()
    pl.semaphore_signal(barrier, inc=1, device_id=(r, other), device_id_type=MESH)
    near = neighbours()
    for _, ahead, behind in near:
        pl.semaphore_signal(barrier, inc=1, device_id=(ahead, core), device_id_type=MESH)
        pl.semaphore_signal(barrier, inc=1, device_id=(behind, core), device_id_type=MESH)
    pl.semaphore_wait(barrier, 1 + 2 * len(near))

    def push(k, src, dst):
        return pltpu.make_async_remote_copy(
            src_ref=src, dst_ref=dst, send_sem=w_send.at[k], recv_sem=w_recv.at[k],
            device_id=(r, other), device_id_type=MESH,
        )

    def ff_push(j):
        out = []
        for q in range(4):
            cols = pl.ds(pl.multiple_of(q * 1280 + j * 256, 256), 256)
            out.append(push(3 + 5 * j + q, gu_w.at[:, cols], gu_far.at[:, cols]))
        cols = pl.ds(pl.multiple_of(j * 256, 256), 256)
        out.append(push(3 + 5 * j + 4, down_w.at[:, cols], down_far.at[:, cols]))
        return out

    push_gain = push(0, gains, gain_far)
    push_qkv = push(1, qkv_w, wqkv.at[mine480])
    push_out = push(2, out_w, wout.at[mine480])
    push_gain.start()
    push_qkv.start()
    push_out.start()
    for j in range(FF_CHUNKS):
        for c in ff_push(j):
            c.start()

    def loads(j):
        slot = lax.rem(j, 2)
        out = []
        for q in range(4):
            cols = pl.ds(pl.multiple_of(q * 1280 + j * 256, 256), 256)
            for i, (src, rows) in enumerate(((gu_w, mine480), (gu_far, other480))):
                out.append(pltpu.make_async_copy(src.at[:, cols], wg.at[slot, q, rows], load_sem.at[slot, 2 * q + i]))
        cols = pl.ds(pl.multiple_of(j * 256, 256), 256)
        out.append(pltpu.make_async_copy(down_w.at[:, cols], wd.at[slot, core], load_sem.at[slot, 8]))
        out.append(pltpu.make_async_copy(down_far.at[:, cols], wd.at[slot, other], load_sem.at[slot, 9]))
        return out

    def start_loads(j):
        for c in ff_push(j):
            c.wait_recv()
        for c in loads(j):
            c.start()

    lane = lax.broadcasted_iota(jnp.int32, (TOK, LANES), 1)
    low = lane < HEAD_SIZE
    early = lax.rem(lane, HEAD_SIZE) < HEAD_SIZE // 2

    def swap(t):
        return jnp.where(early, pltpu.roll(t, LANES - 32, 1), pltpu.roll(t, 32, 1))

    def rope(t):
        return t * cosine[...] + swap(t) * sine[...]

    def rope_back(t):
        return t * cosine[...] - swap(t) * sine[...]

    def transpose(t):
        return jnp.transpose(t.astype(F32)).astype(BF16)

    line = starts[...].astype(F32)
    row = lax.broadcasted_iota(jnp.int32, (TOK, TOK), 0)
    column = lax.broadcasted_iota(jnp.int32, (TOK, TOK), 1)
    across = jnp.broadcast_to(line, (TOK, TOK))
    down_col = jnp.sum(jnp.where(row == column, across, 0.0), axis=1, keepdims=True)
    bias[...] = jnp.where((down_col == across) & (row >= column), 0.0, HIDDEN)
    position = lax.broadcasted_iota(jnp.int32, (TOK, LANES), 0).astype(F32) - down_col
    index = lax.rem(lane, 32).astype(F32)
    freq = jnp.exp(-jnp.log(jnp.full((TOK, LANES), 10000.0, F32)) * index * 2.0 / HEAD_SIZE)
    angle = position * freq
    cosine[...] = jnp.cos(angle)
    sine[...] = jnp.where(early, -jnp.sin(angle), jnp.sin(angle))

    push_gain.wait_recv()

    def gain(k):
        return (gains[k : k + 1, :].astype(F32) + gain_far[k : k + 1, :].astype(F32))[:, :D]

    def rows_of(i):
        return pl.ds(pl.multiple_of(i * BLOCK, BLOCK), BLOCK)

    def normed(x):
        inv = lax.rsqrt(jnp.mean(x * x, axis=-1, keepdims=True) + EPSILON)
        return x * inv, inv

    copy_tok.wait()
    copy_dy.wait()
    for t in range(8):
        w = min(LANES, D - t * LANES)
        place = slice(t * LANES, t * LANES + w)
        tok[:, place] = transpose(h2t[place, :])
        dyp[:, place] = transpose(dyt[place, :])

    def norm_one(i, _):
        rows = rows_of(i)
        n, _inv = normed(tok[rows, :].astype(F32))
        hbuf[rows, :] = (n * gain(0)).astype(BF16)
        return 0

    lax.fori_loop(0, TOK // BLOCK, norm_one, 0)

    def transposed(dst, src):
        for t in range(8):
            w = min(LANES, D - t * LANES)
            dst[t * LANES : t * LANES + w, :] = transpose(src[:, t * LANES : t * LANES + w])

    transposed(h1t, hbuf)

    own_qkv.wait()
    push_qkv.wait_recv()
    for n0 in range(0, QKV, 256):
        width = min(256, QKV - n0)
        joint = mm(hbuf[...], wqkv[:, n0 : n0 + width])
        for c0 in range(0, width, LANES):
            t = (n0 + c0) // LANES
            if c0 + LANES <= width:
                tile = joint[:, c0 : c0 + LANES]
            else:
                piece = joint[:, c0:width]
                tile = jnp.concatenate([piece, piece], axis=1)
            turned = rope(tile) if t < 10 else tile
            if t < 8:
                flipped = transpose(turned)
                w = min(LANES, D - t * LANES)
                qt[t * LANES : t * LANES + w, :] = flipped[:w]
            for part in range(2):
                b = 2 * t + part
                here = low if part == 0 else jnp.logical_not(low)
                if b < QUERY_HEADS:
                    qs[b] = jnp.where(here, turned, 0.0).astype(BF16)
                elif b < QUERY_HEADS + 2 * KEY_VALUE_HEADS:
                    both = jnp.where(here, turned, pltpu.roll(turned, HEAD_SIZE, 1)).astype(BF16)
                    if b < QUERY_HEADS + KEY_VALUE_HEADS:
                        ks[b - QUERY_HEADS] = both
                    else:
                        vs[b - QUERY_HEADS - KEY_VALUE_HEADS] = both

    def attend(g, _):
        for i in range(GROUP):
            h = GROUP * g + i
            s = mm_nt(qs[h], ks[g]) * SCALE + bias[...]
            e = jnp.exp(s - jnp.max(s, axis=-1, keepdims=True))
            p = (e * (1.0 / jnp.sum(e, axis=-1, keepdims=True))).astype(BF16)
            ps[h] = p
            os[h] = mm(p, vs[g]).astype(BF16)
        return 0

    lax.fori_loop(0, KEY_VALUE_HEADS, attend, 0)

    def pair_tile(t):
        a = os[2 * t].astype(F32)
        if 2 * t + 1 < QUERY_HEADS:
            a = jnp.where(low, a, os[2 * t + 1].astype(F32))
        return a

    for t in range(8):
        w = min(LANES, D - t * LANES)
        tile = pair_tile(t)
        hbuf[:, t * LANES : t * LANES + w] = tile[:, :w].astype(BF16)
        ot[t * LANES : t * LANES + w, :] = jnp.transpose(tile).astype(BF16)[:w]

    own_out.wait()
    push_out.wait_recv()
    for n0 in range(0, D, 256):
        cols = slice(n0, min(D, n0 + 256))
        x1[:, cols] = tok[:, cols].astype(F32) + mm(hbuf[...], wout[:, cols])

    start_loads(0)
    start_loads(1)

    def norm_two(i, _):
        rows = rows_of(i)
        x = x1[rows, :]
        n, _inv = normed(x)
        hbuf[rows, :] = (n * gain(1)).astype(BF16)
        yacc[rows, :] = x
        dh2[rows, :] = jnp.zeros((BLOCK, D), F32)
        return 0

    lax.fori_loop(0, TOK // BLOCK, norm_two, 0)
    transposed(h2t, hbuf)

    def pair(k, slot, first, count, base):
        return pltpu.make_async_remote_copy(
            src_ref=box.at[slot, other, pl.ds(first, count)],
            dst_ref=work.at[pl.ds(base + first, count)],
            send_sem=pair_send.at[k],
            recv_sem=pair_recv.at[k],
            device_id=(r, other),
            device_id_type=MESH,
        )

    def tile_columns(slot, half, at, value, count):
        for c in range(count):
            block = value[:, c * LANES : (c + 1) * LANES]
            n = block.shape[0] // ROWS
            box[slot, half, pl.ds(at + c * n, n)] = block.astype(BF16).reshape(n, ROWS, LANES)

    def folded(value):
        n = value.shape[0] // 2
        left = lax.broadcasted_iota(jnp.int32, (n, LANES), 1) < HEAD_SIZE
        return jnp.where(left, value[:n], value[n:])

    def feed_forward(tick):
        j, s = lax.div(tick, 2), lax.rem(tick, 2)
        slot = lax.rem(j, 2)

        @pl.when(s == 0)
        def _():
            for c in loads(j):
                c.wait()

        gate = mm(hbuf[...], wg[slot, s])
        upper = mm(hbuf[...], wg[slot, 2 + s])
        grad = mm(dyp[:, :D], wd[slot, s])
        sigma = jax.nn.sigmoid(gate)
        silu = gate * sigma
        inner_low = (silu * upper).astype(BF16)
        dgate = (grad * upper * sigma * (1.0 + gate * (1.0 - sigma))).astype(BF16)
        dupper = (grad * silu).astype(BF16)
        yacc[...] += mm_nt(inner_low, wd[slot, s])
        dh2[...] += mm_nt(dgate, wg[slot, s]) + mm_nt(dupper, wg[slot, 2 + s])
        for half in range(2):
            left = h2t[half * HALF : (half + 1) * HALF, :]
            tile_columns(slot, half, s * 120, mm(left, dgate), 2)
            tile_columns(slot, half, s * 120 + 60, mm(left, dupper), 2)
        tile_columns(slot, s, 240, mm(dyt[...], inner_low), 2)

        @pl.when(s == 1)
        def _():
            pair(j, slot, 0, FF_USED, j * FF_TILES).start()

            @pl.when(j + 2 < FF_CHUNKS)
            def _():
                start_loads(j + 2)

    def gain_rows(value):
        return jnp.sum(value.reshape(BLOCK // 8, 8, D), axis=0)

    def output_projection():
        gacc2[...] = jnp.zeros((8, D), F32)

        def back_two(i, _):
            rows = rows_of(i)
            n, inv = normed(x1[rows, :])
            d = dh2[rows, :]
            gacc2[...] += gain_rows(d * n)
            dn = d * gain(1)
            dx = dyp[rows, :D].astype(F32) + inv * (dn - n * jnp.mean(dn * n, axis=-1, keepdims=True))
            dh2[rows, :] = dx
            da = dx.astype(BF16)
            dyp[rows, : 7 * LANES] = da[:, : 7 * LANES]
            last = da[:, 7 * LANES :]
            dyp[rows, 7 * LANES :] = jnp.concatenate([last, last], axis=1)
            return 0

        lax.fori_loop(0, TOK // BLOCK, back_two, 0)
        transposed(h2t, yacc)
        pltpu.make_async_copy(h2t, mixed, out_sem.at[0]).start()
        for half in range(2):
            v = mm(ot[half * HALF : (half + 1) * HALF, :], dyp[...])
            tile_columns(1, half, 0, v, 7)
            tile_columns(1, half, 210, folded(v[:, 7 * LANES :]), 1)
        pair(5, 1, 0, OUT_USED, OUT_BASE).start()
        for n0 in range(0, D, 256):
            width = min(256, D - n0)
            v = mm_nt(dyp[:, :D], wout[n0 : n0 + width, :])
            for c0 in range(0, width, LANES):
                t = (n0 + c0) // LANES
                if c0 + LANES <= width:
                    tile = v[:, c0 : c0 + LANES]
                else:
                    piece = v[:, c0:width]
                    tile = jnp.concatenate([piece, piece], axis=1)
                w = min(LANES, D - t * LANES)
                dot_[t * LANES : t * LANES + w, :] = transpose(tile)[:w]
                qs[2 * t] = jnp.where(low, tile, 0.0).astype(BF16)
                if 2 * t + 1 < QUERY_HEADS:
                    qs[2 * t + 1] = jnp.where(low, 0.0, tile).astype(BF16)

    def attend_back(g):
        key_t = jnp.zeros((HEAD_SIZE, TOK), F32)
        value_t = jnp.zeros((HEAD_SIZE, TOK), F32)
        for i in range(GROUP):
            h = GROUP * g + i
            dp = mm_nt(qs[h], vs[g])
            low_p = ps[h]
            p = low_p.astype(F32)
            delta = jnp.sum(dp * p, axis=-1, keepdims=True)
            ds = (p * (dp - delta)).astype(BF16)
            os[h] = rope_back(mm(ds, ks[g]) * SCALE).astype(BF16)
            rows = pl.ds(pl.multiple_of(h * HEAD_SIZE, HEAD_SIZE), HEAD_SIZE)
            key_t = key_t + mm(qt[rows, :], ds)
            value_t = value_t + mm(dot_[rows, :], low_p)
        kvt[pl.ds(pl.multiple_of(HEAD_SIZE * (1 + g), HEAD_SIZE), HEAD_SIZE), :] = key_t * SCALE
        kvt[pl.ds(pl.multiple_of(HEAD_SIZE * (6 + g), HEAD_SIZE), HEAD_SIZE), :] = value_t
        kvt[HEAD_SIZE * 11 : HEAD_SIZE * 12, :] = value_t

    def joint_projection():
        for t in range(13):
            if t < 7:
                tile = pair_tile(t)
            else:
                tile = jnp.transpose(kvt[(t - 7) * LANES : (t - 6) * LANES, :])
                if t < 10:
                    tile = rope_back(tile)
                if t == 7:
                    tile = jnp.where(low, pair_tile(7), tile)
            dqkv[:, t * LANES : (t + 1) * LANES] = tile.astype(BF16)
        for half in range(2):
            left = h1t[half * HALF : (half + 1) * HALF, :]
            for n0 in range(0, 1536, 256):
                v = mm(left, dqkv[:, n0 : n0 + 256])
                tile_columns(0, half, n0 // LANES * 30, v, 2)
            v = mm(left, dqkv[:, 1536:])
            tile_columns(0, half, 360, folded(v), 1)
        pair(6, 0, 0, QKV_USED, QKV_BASE).start()
        for n0 in range(0, D, 256):
            cols = slice(n0, min(D, n0 + 256))
            yacc[:, cols] = mm_nt(dqkv[:, :QKV], wqkv[cols, :])
        gacc1[...] = jnp.zeros((8, D), F32)

        def back_one(i, _):
            rows = rows_of(i)
            n, inv = normed(tok[rows, :].astype(F32))
            d = yacc[rows, :]
            gacc1[...] += gain_rows(d * n)
            dn = d * gain(0)
            dh2[rows, :] += inv * (dn - n * jnp.mean(dn * n, axis=-1, keepdims=True))
            return 0

        lax.fori_loop(0, TOK // BLOCK, back_one, 0)
        for t in range(8):
            place = slice(t * LANES, min(D, (t + 1) * LANES))
            kvt[place, :] = jnp.transpose(dh2[:, place])
        pltpu.make_async_copy(kvt, input_grad, out_sem.at[1]).start()
        gain_sum[...] = jnp.zeros((ROWS, LANES), F32)
        for k, acc in enumerate((gacc1, gacc2)):
            total = jnp.sum(acc[...], axis=0, keepdims=True)
            for t in range(8):
                w = min(LANES, D - t * LANES)
                gain_sum[8 * k + t : 8 * k + t + 1, :w] = total[:, t * LANES : t * LANES + w]
        for half in range(2):
            box[0, half, GAIN_TILE] = gain_sum[...].astype(BF16)
        pair(7, 0, GAIN_TILE, 1, QKV_BASE).start()

    def add_own(slot, base, count):
        def step(i, _):
            o = i * 5
            total = work[pl.ds(base + o, 5)].astype(F32) + box[slot, core, pl.ds(o, 5)].astype(F32)
            work[pl.ds(base + o, 5)] = total.astype(BF16)
            return 0

        lax.fori_loop(0, count // 5, step, 0)

    ff_travel = functools.partial(Travel, work, extra, result, sems)

    def of_ff(g):
        return ff_travel(g, g * FF_TILES, g * FF_EXTRA, UNITS)

    of_out = ff_travel(5, OUT_BASE, OUT_EXTRA_BASE, OUT_UNITS)
    of_qkv = ff_travel(6, QKV_BASE, QKV_EXTRA_BASE, UNITS)

    def travel(tick):
        for k in range(STEPS - 1, -1, -1):
            since = tick - 2 - k

            @pl.when((since >= 0) & (since <= 2 * FF_CHUNKS - 2) & (lax.rem(since + 64, 2) == 0))
            def _(k=k, since=since):
                g = lax.div(since, 2)
                if k == 0:
                    c = pair(g, lax.rem(g, 2), 0, FF_USED, g * FF_TILES)
                    c.wait()
                    add_own(lax.rem(g, 2), g * FF_TILES, FF_USED)
                of_ff(g).step(k)

        @pl.when(tick > OUT_TICK)
        def _():
            for k in range(STEPS):

                @pl.when(tick == OUT_TICK + 1 + k)
                def _(k=k):
                    if k == 0:
                        pair(5, 1, 0, OUT_USED, OUT_BASE).wait()
                        add_own(1, OUT_BASE, OUT_USED)
                    of_out.step(k)

        @pl.when(tick > LAST_TICK)
        def _():
            for k in range(STEPS):

                @pl.when(tick == LAST_TICK + 1 + k)
                def _(k=k):
                    if k == 0:
                        pair(6, 0, 0, QKV_USED, QKV_BASE).wait()
                        add_own(0, QKV_BASE, QKV_USED)
                        pair(7, 0, GAIN_TILE, 1, QKV_BASE).wait()
                        at = QKV_BASE + GAIN_TILE
                        work[at] = (work[at].astype(F32) + box[0, core, GAIN_TILE].astype(F32)).astype(BF16)
                    of_qkv.step(k)

    def tick_body(tick, _):
        @pl.when(tick < OUT_TICK)
        def _():
            feed_forward(tick)

        @pl.when(tick == OUT_TICK)
        def _():
            output_projection()

        @pl.when((tick >= ATTN_TICK) & (tick < LAST_TICK))
        def _():
            attend_back(tick - ATTN_TICK)

        @pl.when(tick == LAST_TICK)
        def _():
            joint_projection()

        travel(tick)
        return 0

    lax.fori_loop(0, TICKS, tick_body, 0)

    pltpu.make_async_copy(h2t, mixed, out_sem.at[0]).wait()
    pltpu.make_async_copy(kvt, input_grad, out_sem.at[1]).wait()
    push_gain.wait_send()
    push_qkv.wait_send()
    push_out.wait_send()

    def finish(g, _):
        for c in ff_push(g):
            c.wait_send()
        of_ff(g).finish()
        return 0

    lax.fori_loop(0, FF_CHUNKS, finish, 0)
    of_out.finish()
    of_qkv.finish()


def layer(tokens, starts, out_grad, gains, qkv_w, out_w, gu_w, down_w):
    vm = pltpu.VMEM
    dma = pltpu.SemaphoreType.DMA
    hbm = pl.BlockSpec(memory_space=pl.ANY)
    near = pl.BlockSpec(memory_space=pltpu.VMEM)
    shape = jax.ShapeDtypeStruct
    return pl.pallas_call(
        layer_kernel,
        out_shape=[
            shape((D, TOK), BF16),
            shape((D, TOK), F32),
            shape((TILES, ROWS, LANES), BF16),
            shape((HALF, 2 * FF), BF16),
            shape((D, FF // 2), BF16),
        ],
        in_specs=[hbm, near, hbm, near, hbm, hbm, hbm, hbm],
        out_specs=[hbm] * 5,
        scratch_shapes=[
            vm((TOK, D), BF16),
            vm((D, TOK), BF16),
            vm((TOK, 1024), BF16),
            vm((16, 1024), BF16),
            vm((D, QKV), BF16),
            vm((D, D), BF16),
            vm((2, 4, D, 256), BF16),
            vm((2, 2, D, 256), BF16),
            vm((TOK, LANES), F32),
            vm((TOK, LANES), F32),
            vm((TOK, TOK), F32),
            vm((TOK, D), BF16),
            vm((D, TOK), BF16),
            vm((D, TOK), BF16),
            vm((QUERY_HEADS, TOK, LANES), BF16),
            vm((KEY_VALUE_HEADS, TOK, LANES), BF16),
            vm((KEY_VALUE_HEADS, TOK, LANES), BF16),
            vm((QUERY_HEADS, TOK, TOK), BF16),
            vm((QUERY_HEADS, TOK, LANES), BF16),
            vm((D, TOK), BF16),
            vm((D, TOK), BF16),
            vm((D, TOK), BF16),
            vm((TOK, D), F32),
            vm((TOK, D), F32),
            vm((TOK, D), F32),
            vm((D, TOK), F32),
            vm((TOK, 13 * LANES), BF16),
            vm((8, D), F32),
            vm((8, D), F32),
            vm((ROWS, LANES), F32),
            vm((2, 2, BOX, ROWS, LANES), BF16),
            vm((TILES, ROWS, LANES), BF16),
            vm((EXTRA, ROWS, LANES), BF16),
            dma((2,)), dma((2,)), dma((2, 10)),
            dma((28,)), dma((28,)), dma((8,)), dma((8,)), dma((2,)),
            dma((7, 54)), dma((7, 54)), dma((7, 36)), dma((7, 36)), dma((7, 3)),
        ],
        compiler_params=pltpu.CompilerParams(
            collective_id=0, has_side_effects=True, vmem_limit_bytes=VMEM_LIMIT
        ),
        name="layer",
    )(tokens, starts, out_grad, gains, qkv_w, out_w, gu_w, down_w)


VMEM_LIMIT = 64 * 1024 * 1024 - 256 * 1024


def widen_kernel(
    res, mixed_in, grad_in, down, gu, qkv, out, gain, mixed, grad,
    rv, down_v, gu_v, qkv_v, out_v, in_sem, out_sem, pass_sem,
):
    bounds = [FF_TILES * j for j in range(FF_CHUNKS)] + [OUT_BASE, QKV_BASE]
    counts = [FF_USED] * FF_CHUNKS + [OUT_USED, QKV_USED + 1]
    loads = [
        pltpu.make_async_copy(res.at[pl.ds(b, n)], rv.at[pl.ds(b, n)], in_sem.at[i])
        for i, (b, n) in enumerate(zip(bounds, counts))
    ]
    for c in loads:
        c.start()
    passed = [
        pltpu.make_async_copy(mixed_in, mixed, pass_sem.at[0]),
        pltpu.make_async_copy(grad_in, grad, pass_sem.at[1]),
    ]
    for c in passed:
        c.start()
    stores = []

    def store(src, dst):
        c = pltpu.make_async_copy(src, dst, out_sem.at[len(stores)])
        c.start()
        stores.append(c)

    def column(at, n):
        return rv[pl.ds(at, n)].astype(F32).reshape(n * ROWS, LANES)

    def last_column(at, n):
        both = column(at, n)
        return both[:, :HEAD_SIZE], pltpu.roll(both, HEAD_SIZE, 1)[:, :HEAD_SIZE]

    for j in range(FF_CHUNKS):
        loads[j].wait()
        base = FF_TILES * j
        for s in range(2):
            for w in range(2):
                first = w * FF + s * 1280 + j * 256
                for c in range(2):
                    gu_v[:, first + c * LANES : first + (c + 1) * LANES] = column(base + (s * 2 + w) * 60 + c * 30, 30)
                cols = pl.ds(first, 256)
                store(gu_v.at[:, cols], gu.at[:, cols])
        first = 256 * j
        for c in range(2):
            down_v[:, first + c * LANES : first + (c + 1) * LANES] = column(base + 240 + c * 60, 60)
        cols = pl.ds(first, 256)
        store(down_v.at[:, cols], down.at[:, cols])
    loads[5].wait()
    for c in range(7):
        out_v[:, c * LANES : (c + 1) * LANES] = column(OUT_BASE + c * 30, 30)
    a, b = last_column(OUT_BASE + 210, 15)
    out_v[:240, 7 * LANES :] = a
    out_v[240:, 7 * LANES :] = b
    store(out_v, out)
    loads[6].wait()
    for c in range(12):
        qkv_v[:, c * LANES : (c + 1) * LANES] = column(QKV_BASE + c * 30, 30)
    a, b = last_column(QKV_BASE + 360, 15)
    qkv_v[:240, 12 * LANES :] = a
    qkv_v[240:, 12 * LANES :] = b
    store(qkv_v, qkv)
    gain[...] = rv[QKV_BASE + GAIN_TILE].astype(F32)
    for c in stores:
        c.wait()
    for c in passed:
        c.wait()


def widened(result, mixed, grad):
    vm = pltpu.VMEM
    dma = pltpu.SemaphoreType.DMA
    hbm = pl.BlockSpec(memory_space=pl.ANY)
    shape = jax.ShapeDtypeStruct
    sizes = [(D, FF // 2), (HALF, 2 * FF), (HALF, QKV), (HALF, D)]
    return pl.pallas_call(
        widen_kernel,
        out_shape=[shape(s, F32) for s in sizes]
        + [shape((ROWS, LANES), F32), shape((D, TOK), BF16), shape((D, TOK), F32)],
        in_specs=[hbm] * 3,
        out_specs=[hbm] * 4 + [pl.BlockSpec(memory_space=vm), hbm, hbm],
        scratch_shapes=[
            vm((TILES, ROWS, LANES), BF16),
            *[vm(s, F32) for s in sizes],
            dma((7,)), dma((27,)), dma((2,)),
        ],
        compiler_params=pltpu.CompilerParams(vmem_limit_bytes=48 * 1024 * 1024),
        name="widen",
    )(result, mixed, grad)


def per_device(
    tokens, starts, out_grad, norm_attn, norm_mlp, qkv_weight, out_weight, gate_up_weight, down_weight
):
    core = lax.axis_index("shard")
    both = jnp.stack([norm_attn, norm_mlp])
    gains = jnp.where(
        core == 0, jnp.pad(both, ((0, 14), (0, 544))), jnp.pad(both, ((0, 14), (HALF, 64)))
    )
    mixed, input_grad, result, _, _ = layer(
        tokens.T, starts.reshape(1, TOK), out_grad.T, gains, qkv_weight, out_weight, gate_up_weight, down_weight.T
    )
    down, gu, qkv, out, gain, mixed, input_grad = widened(result, mixed, input_grad)
    first = core * HALF
    gain_one = lax.dynamic_slice(gain[:8].reshape(1024), (first,), (HALF,))
    gain_two = lax.dynamic_slice(gain[8:].reshape(1024), (first,), (HALF,))
    return mixed.T, input_grad.T, gain_one, gain_two, qkv, out, gu, down.T


def solution(mesh):
    rows, weights = P(("replica", "shard"), None), P("shard", None)
    return jax.shard_map(
        per_device,
        mesh=mesh,
        in_specs=(
            rows, P(("replica", "shard")), rows, P("shard"), P("shard"), weights, weights, weights, weights,
        ),
        out_specs=(rows, rows, P("shard"), P("shard"), weights, weights, weights, weights),
        check_vma=False,
    )
```

time: 1210 us -> 198 us (0.16); the launches traced: 1200 us -> 198 us
  waiting for transfers between devices: 423 us -> 0 us
  blocking collectives: 352 us -> 0 us
  local copies, waits for them, and re-layouts: 270 us -> 6.4 us
  Pallas kernels: 0 us -> 190 us
  matrix products: 105 us -> 0 us
  other arithmetic: 29.2 us -> 0.71 us
  between operations: 16.5 us -> 0.68 us
    reduce_scatter x3 -> x0, waiting for transfers between devices: 395 us -> none  [the longest x1 395 us: sum_together(): lax.psum_scatter(lines, axis, tiled=True).reshape(-1)]
    all_gather x2 -> x0, blocking collectives: 347 us -> none  [the longest x1 176 us: per_device(): lax.all_gather(reduced[3].astype(jnp.bfloat16), 'replica', axis=1, tiled=...]
    pallas_call x0 -> x2, Pallas kernels: none -> 190 us  [the longest x1 179 us: layer(): pl.pallas_call(layer_kernel, out_shape=[shape((D, TOK), BF16), shape((D,...]
    dot_general x17 -> x0, matrix products: 98 us -> none  [the longest x4 18.5 us: transpose_dot(): jnp.einsum('ta,tb->ab', left, right, preferred_element_type=jnp.float32)]
    reshape x13 -> x2, local copies, waits for them, and re-layouts: 84.3 us -> 1.25 us  [the longest x1 1.25 us: per_device(): starts.reshape(1, TOK)]
    unnamed x78 -> x4, local copies, waits for them, and re-layouts: 67.9 us -> 2.48 us
    concatenate x3 -> x0, local copies, waits for them, and re-layouts: 56.1 us -> none  [the longest x1 26 us: sent_together(): both = jnp.concatenate(columns, axis=along)]
    slice x14 -> x0, local copies, waits for them, and re-layouts: 27.7 us -> none  [the longest x7 27.2 us: sent_together(): piece = filled[..., at:at + column.shape[along]]]
  transfers between devices with their start and end apart: 8 -> 0, of which waited for: 2 -> 0; matrix products, arithmetic and copies ran while one was open for 15% -> 0% of each run, Pallas kernels for 0% -> 0%
where the time goes in v1:
time: 198 us
  Pallas kernels  190 us (96%)
  local copies, waits for them, and re-layouts  6.4 us (3%)
    pallas_call x1, Pallas kernels, layer(): pl.pallas_call(layer_kernel, out_shape=[shape((D, TOK), BF16), shape((D,...  179 us
    pallas_call x1, Pallas kernels, widened(): pl.pallas_call(widen_kernel, out_shape=[shape(s, F32) for s in sizes] + [...  10.4 us

profile of v1, /device:TPU:0, one launch (start us, length us, event | category | flops | bytes accessed | tf_op | source)
XLA Modules:
  0.0 197.5 jit_solution(10927562838976094950)
XLA Ops:
  0.6 1.2 reshape.25.starts
  1.9 0.7 stack.9
  2.6 0.7 stack.10
  3.3 0.7 pad_select_fusion.gains
  4.0 179.3 %layer.1 = (bf16[960,384]{1,0:T(8,128)(2,1)}, f32[960,384]{1,0:T(8,128)}, bf16[2560,16,128]{2,1,0:T(8,128)(2,1)}, bf16[480,5120]{1,0:T(8,128)(2,1)}, bf16[960,1280]{1,0:T(8,128)(2,1)}) custom-call(bf16[960,384]{1,0:T(8,128)(2,1)} %bitcast.11, s32[1,384]{1,0:T(1,128)} %reshape.25.starts, bf16[960,384]{1,0:T(8,128)(2,1)} %bitcast.12, ...), custom_call_target="tpu_custom_call" | custom-call | tf_op jit(solution)/shard_map/layer/pallas_call | solution.py:694
  183.3 0.0 copy-start
  183.3 1.4 copy-done
  184.6 0.0 copy-start.1
  184.6 1.1 copy-done.1
  185.8 10.4 %widen.1 = (f32[960,1280]{1,0:T(8,128)}, f32[480,5120]{1,0:T(8,128)}, f32[480,1600]{1,0:T(8,128)}, f32[480,960]{1,0:T(8,128)}, f32[16,128]{1,0:T(8,128)S(1)}, /*...) custom-call(bf16[2560,16,128]{2,1,0:T(8,128)(2,1)} %get-tuple-element.18.res, bf16[960,384]{1,0:T(8,128)(2,1)S(1)} %copy-done.1, ...), custom_call_target="tpu_custom_call" | custom-call | tf_op jit(solution)/shard_map/widen/pallas_call | solution.py:827
  196.2 0.7 dynamic_slice.7
  196.9 0.6 dynamic_slice.6
  (2 shorter events, 0.0 us)
Async XLA Ops:
  183.3 1.4 copy-start
  184.6 1.1 copy-start.1

commit v2 on v1

--- a/solution.py
+++ b/solution.py
@@ -45,12 +45,19 @@
 OUT_EXTRA_BASE = FF_CHUNKS * FF_EXTRA
 QKV_EXTRA_BASE = OUT_EXTRA_BASE + 252
 EXTRA = QKV_EXTRA_BASE + FF_EXTRA
-STEPS = 13
+FF_HOPS = (2, 1, 1)
+OUT_HOPS = (2, 1, 1)
+QKV_HOPS = (2, 1, 1)
+
+
+def steps_of(hops):
+    return 7 + 2 * sum(h - 1 for h in hops)
+
 
 OUT_TICK = 2 * FF_CHUNKS
 ATTN_TICK = OUT_TICK + 1
 LAST_TICK = ATTN_TICK + KEY_VALUE_HEADS
-TICKS = LAST_TICK + 1 + STEPS
+TICKS = max(2 * FF_CHUNKS + 2 * steps_of(FF_HOPS) - 1, LAST_TICK + 1 + steps_of(QKV_HOPS))
 
 
 def mm(a, b):
@@ -70,7 +77,8 @@
     for place, stride in ((x, 1), (y, 4), (z, 16)):
         ahead = r + stride * (lax.rem(place + 1, 4) - place)
         behind = r + stride * (lax.rem(place + 3, 4) - place)
-        out.append((place, ahead, behind))
+        across = r + stride * (lax.rem(place + 2, 4) - place)
+        out.append((place, ahead, behind, across))
     return out
 
 
@@ -92,9 +100,10 @@
 
 
 class Travel:
-    def __init__(self, work, extra, result, sems, group, base, extra_base, units):
-        self.work, self.extra, self.result, self.group = work, extra, result, group
-        self.send, self.recv, self.back_send, self.back_recv, self.keep_sem = sems
+    def __init__(self, work, extra, result, sems, group, base, extra_base, units, hops):
+        self.work, self.extra, self.result = work, extra, result
+        send, recv, back_send, back_recv, keep_sem = sems
+        self.hops = hops
         core = lax.axis_index("shard")
         near = neighbours()
         self.there, self.back, self.keeps = [[], [], []], [[], [], []], []
@@ -102,7 +111,7 @@
             seg = base + 64 * n * color
             at = extra_base + 63 * n * color
             for phase in range(3):
-                place, ahead, behind = near[(color + phase) % 3]
+                place, ahead, behind, across = near[(color + phase) % 3]
                 chunk = (16, 4, 1)[phase] * n
                 first = chunk // 2
                 second = chunk - first
@@ -115,102 +124,154 @@
 
                 def out(k, src, count, dst, to, color=color, phase=phase):
                     index = color * 18 + phase * 6 + k
-                    return pltpu.make_async_remote_copy(
+                    return lambda: pltpu.make_async_remote_copy(
                         src_ref=work.at[pl.ds(src, count)],
                         dst_ref=extra.at[pl.ds(dst, count)],
-                        send_sem=self.send.at[group, index],
-                        recv_sem=self.recv.at[group, index],
+                        send_sem=send.at[group, index],
+                        recv_sem=recv.at[group, index],
                         device_id=(to, core),
                         device_id_type=MESH,
                     )
 
                 def home(k, source, at, count, to, color=color, phase=phase):
                     index = color * 12 + phase * 4 + k
-                    return pltpu.make_async_remote_copy(
+                    return lambda: pltpu.make_async_remote_copy(
                         src_ref=source.at[pl.ds(at, count)],
                         dst_ref=result.at[pl.ds(at, count)],
-                        send_sem=self.back_send.at[group, index],
-                        recv_sem=self.back_recv.at[group, index],
+                        send_sem=back_send.at[group, index],
+                        recv_sem=back_recv.at[group, index],
                         device_id=(to, core),
                         device_id_type=MESH,
                     )
 
-                self.there[phase].append((
-                    (
-                        lambda out=out, far=far, first=first, xa=xa, to=ahead: out(0, far, first, xa, to),
-                        lambda out=out, far=far, first=first, second=second, xb=xb, to=behind: out(1, far + first, second, xb, to),
-                        lambda out=out, plus=plus, first=first, second=second, yp=yp, to=ahead: out(2, plus + first, second, yp + first, to),
-                        lambda out=out, minus=minus, first=first, ym=ym, to=behind: out(3, minus, first, ym, to),
-                        lambda out=out, plus=plus, first=first, yp=yp, to=ahead: out(4, plus, first, yp, to),
-                        lambda out=out, minus=minus, first=first, second=second, ym=ym, to=behind: out(5, minus + first, second, ym + first, to),
-                    ),
-                    (first, second, chunk, xa, xb, yp, ym, mine, plus, minus),
-                ))
                 source = work if phase == 2 else result
-                self.back[phase].append((
-                    lambda home=home, source=source, mine=mine, chunk=chunk, to=ahead: home(0, source, mine, chunk, to),
-                    lambda home=home, source=source, mine=mine, chunk=chunk, to=behind: home(1, source, mine, chunk, to),
-                    lambda home=home, minus=minus, first=first, to=ahead: home(2, result, minus, first, to),
-                    lambda home=home, plus=plus, first=first, second=second, to=behind: home(3, result, plus + first, second, to),
-                ))
+                if hops[phase] == 2:
+                    copies = (
+                        out(0, far, first, xa, ahead),
+                        out(1, far + first, second, xb, behind),
+                        out(2, plus + first, second, yp + first, ahead),
+                        out(3, minus, first, ym, behind),
+                        out(4, plus, first, yp, ahead),
+                        out(5, minus + first, second, ym + first, behind),
+                    )
+                    backs = (
+                        home(0, source, mine, chunk, ahead),
+                        home(1, source, mine, chunk, behind),
+                        home(2, result, minus, first, ahead),
+                        home(3, result, plus + first, second, behind),
+                    )
+                else:
+                    copies = (
+                        out(0, far, chunk, xa, across),
+                        out(1, plus, chunk, yp, ahead),
+                        out(2, minus, chunk, ym, behind),
+                    )
+                    backs = (
+                        home(0, source, mine, chunk, across),
+                        home(1, source, mine, chunk, ahead),
+                        home(2, source, mine, chunk, behind),
+                    )
+                self.there[phase].append((copies, (first, second, chunk, xa, xb, yp, ym, mine, plus, minus)))
+                self.back[phase].append(backs)
                 if phase == 2:
                     self.keeps.append(
                         lambda mine=mine, chunk=chunk, color=color: pltpu.make_async_copy(
                             work.at[pl.ds(mine, chunk)],
                             result.at[pl.ds(mine, chunk)],
-                            self.keep_sem.at[group, color],
+                            keep_sem.at[group, color],
                         )
                     )
                 seg = mine
 
+    def start(self, phase):
+        for c, _ in self.there[phase]:
+            for i in range(4 if self.hops[phase] == 2 else 3):
+                c[i]().start()
+
+    def mid(self, phase):
+        for c, (first, second, chunk, xa, xb, yp, ym, mine, plus, minus) in self.there[phase]:
+            c[0]().wait_recv()
+            add_into(self.work, plus, [(self.extra, xa)], first)
+            c[4]().start()
+            c[1]().wait_recv()
+            add_into(self.work, minus + first, [(self.extra, xb)], second)
+            c[5]().start()
+
+    def end(self, phase, color):
+        c, (first, second, chunk, xa, xb, yp, ym, mine, plus, minus) = self.there[phase][color]
+        terms = [(self.extra, yp), (self.extra, ym)]
+        if self.hops[phase] == 2:
+            waits = c[2:]
+        else:
+            waits = c
+            terms.append((self.extra, xa))
+        for w in waits:
+            w().wait_recv()
+        add_into(self.work, mine, terms, chunk)
+
+    def back_start(self, phase, color):
+        c = self.back[phase][color]
+        for i in range(2 if self.hops[phase] == 2 else 3):
+            c[i]().start()
+        if phase == 2:
+            self.keeps[color]().start()
+
+    def back_mid(self, phase):
+        for c in self.back[phase]:
+            c[0]().wait_recv()
+            c[2]().start()
+            c[1]().wait_recv()
+            c[3]().start()
+
+    def back_end(self, phase, color):
+        c = self.back[phase][color]
+        for w in c[2:] if self.hops[phase] == 2 else c:
+            w().wait_recv()
+        if phase == 2:
+            self.keeps[color]().wait()
+
     def step(self, k):
-        if k < 6 and k % 2 == 1:
-            for c, (first, second, chunk, xa, xb, yp, ym, mine, plus, minus) in self.there[k // 2]:
-                c[0]().wait_recv()
-                add_into(self.work, plus, [(self.extra, xa)], first)
-                c[4]().start()
-                c[1]().wait_recv()
-                add_into(self.work, minus + first, [(self.extra, xb)], second)
-                c[5]().start()
+        colors = range(len(self.keeps))
+        steps = [[("start", 0)]]
+        for phase in range(3):
+            if self.hops[phase] == 2:
+                steps.append([("mid", phase)])
+            steps.append([("turn", phase)])
+        for phase in (2, 1, 0):
+            if self.hops[phase] == 2:
+                steps.append([("back_mid", phase)])
+            steps.append([("back_turn", phase)])
+        if k >= len(steps):
             return
-        if k in (2, 4, 6):
-            for c, (first, second, chunk, xa, xb, yp, ym, mine, plus, minus) in self.there[k // 2 - 1]:
-                for i in (2, 3, 4, 5):
-                    c[i]().wait_recv()
-                add_into(self.work, mine, [(self.extra, yp), (self.extra, ym)], chunk)
-        if k in (0, 2, 4):
-            for c, _ in self.there[k // 2]:
-                for i in (0, 1, 2, 3):
-                    c[i]().start()
-        if k in (7, 9, 11):
-            phase = (11 - k) // 2
-            for n, c in enumerate(self.back[phase]):
-                c[0]().wait_recv()
-                c[2]().start()
-                c[1]().wait_recv()
-                c[3]().start()
-                if phase == 2:
-                    self.keeps[n]().wait()
-        if k in (8, 10, 12):
-            for c in self.back[(12 - k) // 2]:
-                c[2]().wait_recv()
-                c[3]().wait_recv()
-        if k in (6, 8, 10):
-            phase = (10 - k) // 2
-            for n, c in enumerate(self.back[phase]):
-                c[0]().start()
-                c[1]().start()
-                if phase == 2:
-                    self.keeps[n]().start()
+        for kind, phase in steps[k]:
+            if kind == "start":
+                self.start(phase)
+            elif kind == "mid":
+                self.mid(phase)
+            elif kind == "back_mid":
+                self.back_mid(phase)
+            elif kind == "turn":
+                for color in colors:
+                    self.end(phase, color)
+                    if phase < 2:
+                        for i in range(4 if self.hops[phase + 1] == 2 else 3):
+                            self.there[phase + 1][color][0][i]().start()
+                    else:
+                        self.back_start(2, color)
+            else:
+                for color in colors:
+                    self.back_end(phase, color)
+                    if phase > 0:
+                        self.back_start(phase - 1, color)
 
     def finish(self):
         for phase in range(3):
             for c, _ in self.there[phase]:
-                for i in range(6):
-                    c[i]().wait_send()
+                for i in c:
+                    i().wait_send()
             for c in self.back[phase]:
-                for i in range(4):
-                    c[i]().wait_send()
+                for i in c:
+                    i().wait_send()
 
 
 def layer_kernel(
@@ -241,10 +302,9 @@
     barrier = pltpu.get_barrier_semaphore()
     pl.semaphore_signal(barrier, inc=1, device_id=(r, other), device_id_type=MESH)
     near = neighbours()
-    for _, ahead, behind in near:
-        pl.semaphore_signal(barrier, inc=1, device_id=(ahead, core), device_id_type=MESH)
-        pl.semaphore_signal(barrier, inc=1, device_id=(behind, core), device_id_type=MESH)
-    pl.semaphore_wait(barrier, 1 + 2 * len(near))
+    for _, *chips in near:
+        for chip in chips:
+            pl.semaphore_signal(barrier, inc=1, device_id=(chip, core), device_id_type=MESH)
 
     def push(k, src, dst):
         return pltpu.make_async_remote_copy(
@@ -260,16 +320,6 @@
         cols = pl.ds(pl.multiple_of(j * 256, 256), 256)
         out.append(push(3 + 5 * j + 4, down_w.at[:, cols], down_far.at[:, cols]))
         return out
-
-    push_gain = push(0, gains, gain_far)
-    push_qkv = push(1, qkv_w, wqkv.at[mine480])
-    push_out = push(2, out_w, wout.at[mine480])
-    push_gain.start()
-    push_qkv.start()
-    push_out.start()
-    for j in range(FF_CHUNKS):
-        for c in ff_push(j):
-            c.start()
 
     def loads(j):
         slot = lax.rem(j, 2)
@@ -318,18 +368,6 @@
     cosine[...] = jnp.cos(angle)
     sine[...] = jnp.where(early, -jnp.sin(angle), jnp.sin(angle))
 
-    push_gain.wait_recv()
-
-    def gain(k):
-        return (gains[k : k + 1, :].astype(F32) + gain_far[k : k + 1, :].astype(F32))[:, :D]
-
-    def rows_of(i):
-        return pl.ds(pl.multiple_of(i * BLOCK, BLOCK), BLOCK)
-
-    def normed(x):
-        inv = lax.rsqrt(jnp.mean(x * x, axis=-1, keepdims=True) + EPSILON)
-        return x * inv, inv
-
     copy_tok.wait()
     copy_dy.wait()
     for t in range(8):
@@ -337,6 +375,28 @@
         place = slice(t * LANES, t * LANES + w)
         tok[:, place] = transpose(h2t[place, :])
         dyp[:, place] = transpose(dyt[place, :])
+
+    pl.semaphore_wait(barrier, 1 + 3 * len(near))
+    push_gain = push(0, gains, gain_far)
+    push_qkv = push(1, qkv_w, wqkv.at[mine480])
+    push_out = push(2, out_w, wout.at[mine480])
+    push_gain.start()
+    push_qkv.start()
+    push_out.start()
+    for j in range(FF_CHUNKS):
+        for c in ff_push(j):
+            c.start()
+    push_gain.wait_recv()
+
+    def gain(k):
+        return (gains[k : k + 1, :].astype(F32) + gain_far[k : k + 1, :].astype(F32))[:, :D]
+
+    def rows_of(i):
+        return pl.ds(pl.multiple_of(i * BLOCK, BLOCK), BLOCK)
+
+    def normed(x):
+        inv = lax.rsqrt(jnp.mean(x * x, axis=-1, keepdims=True) + EPSILON)
+        return x * inv, inv
 
     def norm_one(i, _):
         rows = rows_of(i)
@@ -382,6 +442,9 @@
                     else:
                         vs[b - QUERY_HEADS - KEY_VALUE_HEADS] = both
 
+    start_loads(0)
+    start_loads(1)
+
     def attend(g, _):
         for i in range(GROUP):
             h = GROUP * g + i
@@ -411,9 +474,6 @@
     for n0 in range(0, D, 256):
         cols = slice(n0, min(D, n0 + 256))
         x1[:, cols] = tok[:, cols].astype(F32) + mm(hbuf[...], wout[:, cols])
-
-    start_loads(0)
-    start_loads(1)
 
     def norm_two(i, _):
         rows = rows_of(i)
@@ -603,16 +663,17 @@
     ff_travel = functools.partial(Travel, work, extra, result, sems)
 
     def of_ff(g):
-        return ff_travel(g, g * FF_TILES, g * FF_EXTRA, UNITS)
-
-    of_out = ff_travel(5, OUT_BASE, OUT_EXTRA_BASE, OUT_UNITS)
-    of_qkv = ff_travel(6, QKV_BASE, QKV_EXTRA_BASE, UNITS)
+        return ff_travel(g, g * FF_TILES, g * FF_EXTRA, UNITS, FF_HOPS)
+
+    of_out = ff_travel(5, OUT_BASE, OUT_EXTRA_BASE, OUT_UNITS, OUT_HOPS)
+    of_qkv = ff_travel(6, QKV_BASE, QKV_EXTRA_BASE, UNITS, QKV_HOPS)
 
     def travel(tick):
-        for k in range(STEPS - 1, -1, -1):
-            since = tick - 2 - k
-
-            @pl.when((since >= 0) & (since <= 2 * FF_CHUNKS - 2) & (lax.rem(since + 64, 2) == 0))
+        for k in range(steps_of(FF_HOPS) - 1, -1, -1):
+            since = tick - 2 - 2 * k
+            turn = lax.rem(since + 64, 4)
+
+            @pl.when((since >= 0) & (since <= 2 * FF_CHUNKS - 2) & ((turn == 0) | (turn == 3)))
             def _(k=k, since=since):
                 g = lax.div(since, 2)
                 if k == 0:
@@ -623,7 +684,7 @@
 
         @pl.when(tick > OUT_TICK)
         def _():
-            for k in range(STEPS):
+            for k in range(steps_of(OUT_HOPS)):
 
                 @pl.when(tick == OUT_TICK + 1 + k)
                 def _(k=k):
@@ -634,7 +695,7 @@
 
         @pl.when(tick > LAST_TICK)
         def _():
-            for k in range(STEPS):
+            for k in range(steps_of(QKV_HOPS)):
 
                 @pl.when(tick == LAST_TICK + 1 + k)
                 def _(k=k):

time: 198 us -> 175 us (0.88)
  Pallas kernels: 190 us -> 167 us
    pallas_call x1, Pallas kernels: 179 us -> 156 us  [layer(): pl.pallas_call(layer_kernel, out_shape=[shape((D, TOK), BF16), shape((D,...]
where the time goes in v2:
time: 175 us
  Pallas kernels  167 us (95%)
  local copies, waits for them, and re-layouts  6.4 us (4%)
    pallas_call x1, Pallas kernels, layer(): pl.pallas_call(layer_kernel, out_shape=[shape((D, TOK), BF16), shape((D,...  156 us
    pallas_call x1, Pallas kernels, widened(): pl.pallas_call(widen_kernel, out_shape=[shape(s, F32) for s in sizes] + [...  10.4 us

profile of v2, /device:TPU:0, one launch (start us, length us, event | category | flops | bytes accessed | tf_op | source)
XLA Modules:
  0.0 174.7 jit_solution(6076928539216723111)
XLA Ops:
  0.6 1.2 reshape.25.starts
  1.9 0.7 stack.9
  2.6 0.7 stack.10
  3.3 0.7 pad_select_fusion.gains
  4.0 156.5 %layer.1 = (bf16[960,384]{1,0:T(8,128)(2,1)}, f32[960,384]{1,0:T(8,128)}, bf16[2560,16,128]{2,1,0:T(8,128)(2,1)}, bf16[480,5120]{1,0:T(8,128)(2,1)}, bf16[960,1280]{1,0:T(8,128)(2,1)}) custom-call(bf16[960,384]{1,0:T(8,128)(2,1)} %bitcast.11, s32[1,384]{1,0:T(1,128)} %reshape.25.starts, bf16[960,384]{1,0:T(8,128)(2,1)} %bitcast.12, ...), custom_call_target="tpu_custom_call" | custom-call | tf_op jit(solution)/shard_map/layer/pallas_call | solution.py:755
  160.4 0.0 copy-start
  160.4 1.4 copy-done
  161.8 0.0 copy-start.1
  161.8 1.1 copy-done.1
  162.9 10.4 %widen.1 = (f32[960,1280]{1,0:T(8,128)}, f32[480,5120]{1,0:T(8,128)}, f32[480,1600]{1,0:T(8,128)}, f32[480,960]{1,0:T(8,128)}, f32[16,128]{1,0:T(8,128)S(1)}, /*...) custom-call(bf16[2560,16,128]{2,1,0:T(8,128)(2,1)} %get-tuple-element.18.res, bf16[960,384]{1,0:T(8,128)(2,1)S(1)} %copy-done.1, ...), custom_call_target="tpu_custom_call" | custom-call | tf_op jit(solution)/shard_map/widen/pallas_call | solution.py:888
  173.4 0.7 dynamic_slice.7
  174.0 0.6 dynamic_slice.6
  (2 shorter events, 0.0 us)
Async XLA Ops:
  160.4 1.4 copy-start
  161.8 1.1 copy-start.1

commit v3 on v2

--- a/solution.py
+++ b/solution.py
@@ -100,16 +100,28 @@
 
 
 class Travel:
-    def __init__(self, work, extra, result, sems, group, base, extra_base, units, hops):
+    def __init__(self, near, core, work, extra, result, sems, group, base, extra_base, units, hops):
         self.work, self.extra, self.result = work, extra, result
         send, recv, back_send, back_recv, keep_sem = sems
-        self.hops = hops
-        core = lax.axis_index("shard")
-        near = neighbours()
+        self.hops, self.units = hops, units
         self.there, self.back, self.keeps = [[], [], []], [[], [], []], []
+        self.sent = 63 * sum(units)
+
+        def copy(src, dst, send_sem, recv_sem, to):
+            return pltpu.make_async_remote_copy(
+                src_ref=src, dst_ref=dst, send_sem=send_sem, recv_sem=recv_sem, device_id=(to, core), device_id_type=MESH
+            )
+
+        partner = near[0][1]
+        self.all_sent = [
+            lambda sem=sem: copy(
+                work.at[pl.ds(0, self.sent)], extra.at[pl.ds(0, self.sent)], sem.at[group], recv.at[group, 0], partner
+            ).wait_send()
+            for sem in (send, back_send)
+        ]
         for color, n in enumerate(units):
-            seg = base + 64 * n * color
-            at = extra_base + 63 * n * color
+            seg = base + 64 * sum(units[:color])
+            at = extra_base + 63 * sum(units[:color])
             for phase in range(3):
                 place, ahead, behind, across = near[(color + phase) % 3]
                 chunk = (16, 4, 1)[phase] * n
@@ -121,27 +133,17 @@
                 far = seg + chunk * lax.rem(place + 2, 4)
                 xa, xb, yp, ym = at, at + first, at + chunk, at + 2 * chunk
                 at = at + 3 * chunk
-
-                def out(k, src, count, dst, to, color=color, phase=phase):
-                    index = color * 18 + phase * 6 + k
-                    return lambda: pltpu.make_async_remote_copy(
-                        src_ref=work.at[pl.ds(src, count)],
-                        dst_ref=extra.at[pl.ds(dst, count)],
-                        send_sem=send.at[group, index],
-                        recv_sem=recv.at[group, index],
-                        device_id=(to, core),
-                        device_id_type=MESH,
+                slot = color * 9 + phase * 3
+
+                def out(k, src, count, dst, to, slot=slot):
+                    return lambda: copy(
+                        work.at[pl.ds(src, count)], extra.at[pl.ds(dst, count)], send.at[group], recv.at[group, slot + k], to
                     )
 
-                def home(k, source, at, count, to, color=color, phase=phase):
-                    index = color * 12 + phase * 4 + k
-                    return lambda: pltpu.make_async_remote_copy(
-                        src_ref=source.at[pl.ds(at, count)],
-                        dst_ref=result.at[pl.ds(at, count)],
-                        send_sem=back_send.at[group, index],
-                        recv_sem=back_recv.at[group, index],
-                        device_id=(to, core),
-                        device_id_type=MESH,
+                def home(k, source, at, count, to, slot=slot):
+                    return lambda: copy(
+                        source.at[pl.ds(at, count)], result.at[pl.ds(at, count)],
+                        back_send.at[group], back_recv.at[group, slot + k], to,
                     )
 
                 source = work if phase == 2 else result
@@ -150,26 +152,30 @@
                         out(0, far, first, xa, ahead),
                         out(1, far + first, second, xb, behind),
                         out(2, plus + first, second, yp + first, ahead),
-                        out(3, minus, first, ym, behind),
-                        out(4, plus, first, yp, ahead),
-                        out(5, minus + first, second, ym + first, behind),
+                        out(2, minus, first, ym, behind),
+                        out(2, plus, first, yp, ahead),
+                        out(2, minus + first, second, ym + first, behind),
+                        out(2, seg, 2 * chunk, yp, ahead),
                     )
                     backs = (
                         home(0, source, mine, chunk, ahead),
                         home(1, source, mine, chunk, behind),
                         home(2, result, minus, first, ahead),
-                        home(3, result, plus + first, second, behind),
+                        home(2, result, plus + first, second, behind),
+                        home(2, result, seg, chunk, ahead),
                     )
                 else:
                     copies = (
                         out(0, far, chunk, xa, across),
-                        out(1, plus, chunk, yp, ahead),
-                        out(2, minus, chunk, ym, behind),
+                        out(0, plus, chunk, yp, ahead),
+                        out(0, minus, chunk, ym, behind),
+                        out(0, seg, 3 * chunk, xa, ahead),
                     )
                     backs = (
                         home(0, source, mine, chunk, across),
-                        home(1, source, mine, chunk, ahead),
-                        home(2, source, mine, chunk, behind),
+                        home(0, source, mine, chunk, ahead),
+                        home(0, source, mine, chunk, behind),
+                        home(0, result, seg, 3 * chunk, ahead),
                     )
                 self.there[phase].append((copies, (first, second, chunk, xa, xb, yp, ym, mine, plus, minus)))
                 self.back[phase].append(backs)
@@ -183,30 +189,25 @@
                     )
                 seg = mine
 
-    def start(self, phase):
-        for c, _ in self.there[phase]:
-            for i in range(4 if self.hops[phase] == 2 else 3):
-                c[i]().start()
-
-    def mid(self, phase):
-        for c, (first, second, chunk, xa, xb, yp, ym, mine, plus, minus) in self.there[phase]:
-            c[0]().wait_recv()
-            add_into(self.work, plus, [(self.extra, xa)], first)
-            c[4]().start()
-            c[1]().wait_recv()
-            add_into(self.work, minus + first, [(self.extra, xb)], second)
-            c[5]().start()
+    def start(self, phase, color):
+        for i in range(4 if self.hops[phase] == 2 else 3):
+            self.there[phase][color][0][i]().start()
+
+    def mid(self, phase, color):
+        c, (first, second, chunk, xa, xb, yp, ym, mine, plus, minus) = self.there[phase][color]
+        c[0]().wait_recv()
+        add_into(self.work, plus, [(self.extra, xa)], first)
+        c[4]().start()
+        c[1]().wait_recv()
+        add_into(self.work, minus + first, [(self.extra, xb)], second)
+        c[5]().start()
 
     def end(self, phase, color):
         c, (first, second, chunk, xa, xb, yp, ym, mine, plus, minus) = self.there[phase][color]
         terms = [(self.extra, yp), (self.extra, ym)]
-        if self.hops[phase] == 2:
-            waits = c[2:]
-        else:
-            waits = c
+        if self.hops[phase] == 1:
             terms.append((self.extra, xa))
-        for w in waits:
-            w().wait_recv()
+        c[-1]().wait_recv()
         add_into(self.work, mine, terms, chunk)
 
     def back_start(self, phase, color):
@@ -216,62 +217,50 @@
         if phase == 2:
             self.keeps[color]().start()
 
-    def back_mid(self, phase):
-        for c in self.back[phase]:
-            c[0]().wait_recv()
-            c[2]().start()
-            c[1]().wait_recv()
-            c[3]().start()
+    def back_mid(self, phase, color):
+        c = self.back[phase][color]
+        c[0]().wait_recv()
+        c[2]().start()
+        c[1]().wait_recv()
+        c[3]().start()
 
     def back_end(self, phase, color):
-        c = self.back[phase][color]
-        for w in c[2:] if self.hops[phase] == 2 else c:
-            w().wait_recv()
+        self.back[phase][color][-1]().wait_recv()
         if phase == 2:
             self.keeps[color]().wait()
 
     def step(self, k):
-        colors = range(len(self.keeps))
-        steps = [[("start", 0)]]
+        steps = [("start", 0)]
         for phase in range(3):
             if self.hops[phase] == 2:
-                steps.append([("mid", phase)])
-            steps.append([("turn", phase)])
+                steps.append(("mid", phase))
+            steps.append(("turn", phase))
         for phase in (2, 1, 0):
             if self.hops[phase] == 2:
-                steps.append([("back_mid", phase)])
-            steps.append([("back_turn", phase)])
-        if k >= len(steps):
-            return
-        for kind, phase in steps[k]:
+                steps.append(("back_mid", phase))
+            steps.append(("back_turn", phase))
+        kind, phase = steps[k]
+        for color in range(len(self.units)):
             if kind == "start":
-                self.start(phase)
+                self.start(phase, color)
             elif kind == "mid":
-                self.mid(phase)
+                self.mid(phase, color)
             elif kind == "back_mid":
-                self.back_mid(phase)
+                self.back_mid(phase, color)
             elif kind == "turn":
-                for color in colors:
-                    self.end(phase, color)
-                    if phase < 2:
-                        for i in range(4 if self.hops[phase + 1] == 2 else 3):
-                            self.there[phase + 1][color][0][i]().start()
-                    else:
-                        self.back_start(2, color)
+                self.end(phase, color)
+                if phase < 2:
+                    self.start(phase + 1, color)
+                else:
+                    self.back_start(2, color)
             else:
-                for color in colors:
-                    self.back_end(phase, color)
-                    if phase > 0:
-                        self.back_start(phase - 1, color)
+                self.back_end(phase, color)
+                if phase > 0:
+                    self.back_start(phase - 1, color)
 
     def finish(self):
-        for phase in range(3):
-            for c, _ in self.there[phase]:
-                for i in c:
-                    i().wait_send()
-            for c in self.back[phase]:
-                for i in c:
-                    i().wait_send()
+        for wait in self.all_sent:
+            wait()
 
 
 def layer_kernel(
@@ -660,7 +649,7 @@
 
         lax.fori_loop(0, count // 5, step, 0)
 
-    ff_travel = functools.partial(Travel, work, extra, result, sems)
+    ff_travel = functools.partial(Travel, near, core, work, extra, result, sems)
 
     def of_ff(g):
         return ff_travel(g, g * FF_TILES, g * FF_EXTRA, UNITS, FF_HOPS)
@@ -799,7 +788,7 @@
             vm((EXTRA, ROWS, LANES), BF16),
             dma((2,)), dma((2,)), dma((2, 10)),
             dma((28,)), dma((28,)), dma((8,)), dma((8,)), dma((2,)),
-            dma((7, 54)), dma((7, 54)), dma((7, 36)), dma((7, 36)), dma((7, 3)),
+            dma((7,)), dma((7, 27)), dma((7,)), dma((7, 27)), dma((7, 3)),
         ],
         compiler_params=pltpu.CompilerParams(
             collective_id=0, has_side_effects=True, vmem_limit_bytes=VMEM_LIMIT
@@ -813,7 +802,7 @@
 
 def widen_kernel(
     res, mixed_in, grad_in, down, gu, qkv, out, gain, mixed, grad,
-    rv, down_v, gu_v, qkv_v, out_v, in_sem, out_sem, pass_sem,
+    rv, down_v, gu_v, qkv_v, out_v, mixed_v, grad_v, in_sem, out_sem, pass_sem,
 ):
     bounds = [FF_TILES * j for j in range(FF_CHUNKS)] + [OUT_BASE, QKV_BASE]
     counts = [FF_USED] * FF_CHUNKS + [OUT_USED, QKV_USED + 1]
@@ -824,8 +813,8 @@
     for c in loads:
         c.start()
     passed = [
-        pltpu.make_async_copy(mixed_in, mixed, pass_sem.at[0]),
-        pltpu.make_async_copy(grad_in, grad, pass_sem.at[1]),
+        pltpu.make_async_copy(mixed_in, mixed_v, pass_sem.at[0]),
+        pltpu.make_async_copy(grad_in, grad_v, pass_sem.at[1]),
     ]
     for c in passed:
         c.start()
@@ -873,9 +862,10 @@
     qkv_v[240:, 12 * LANES :] = b
     store(qkv_v, qkv)
     gain[...] = rv[QKV_BASE + GAIN_TILE].astype(F32)
+    for c, src, dst in zip(passed, (mixed_v, grad_v), (mixed, grad)):
+        c.wait()
+        store(src, dst)
     for c in stores:
-        c.wait()
-    for c in passed:
         c.wait()
 
 
@@ -894,9 +884,11 @@
         scratch_shapes=[
             vm((TILES, ROWS, LANES), BF16),
             *[vm(s, F32) for s in sizes],
-            dma((7,)), dma((27,)), dma((2,)),
+            vm((D, TOK), BF16),
+            vm((D, TOK), F32),
+            dma((7,)), dma((29,)), dma((2,)),
         ],
-        compiler_params=pltpu.CompilerParams(vmem_limit_bytes=48 * 1024 * 1024),
+        compiler_params=pltpu.CompilerParams(vmem_limit_bytes=VMEM_LIMIT),
         name="widen",
     )(result, mixed, grad)
 

time: 175 us -> 166 us (0.949)
  Pallas kernels: 167 us -> 159 us
  local copies, waits for them, and re-layouts: 6.4 us -> 4.6 us
    pallas_call x1, Pallas kernels: 156 us -> 148 us  [layer(): pl.pallas_call(layer_kernel, out_shape=[shape((D, TOK), BF16), shape((D,...]
    unnamed x4 -> x0, local copies, waits for them, and re-layouts: 2.48 us -> none
where the time goes in v3:
time: 166 us; the launch traced here: 165 us
  Pallas kernels  159 us (96%)
  local copies, waits for them, and re-layouts  4.6 us (3%)
    pallas_call x1, Pallas kernels, layer(): pl.pallas_call(layer_kernel, out_shape=[shape((D, TOK), BF16), shape((D,...  148 us
    pallas_call x1, Pallas kernels, widened(): pl.pallas_call(widen_kernel, out_shape=[shape(s, F32) for s in sizes] + [...  11.7 us

profile of v3, /device:TPU:0, one launch (start us, length us, event | category | flops | bytes accessed | tf_op | source)
XLA Modules:
  0.0 165.4 jit_solution(1411289421714494770)
XLA Ops:
  0.6 1.2 reshape.25.starts
  1.9 0.7 stack.9
  2.6 0.7 stack.10
  3.3 0.7 pad_select_fusion.gains
  4.0 147.8 %layer.1 = (bf16[960,384]{1,0:T(8,128)(2,1)}, f32[960,384]{1,0:T(8,128)}, bf16[2560,16,128]{2,1,0:T(8,128)(2,1)}, bf16[480,5120]{1,0:T(8,128)(2,1)}, bf16[960,1280]{1,0:T(8,128)(2,1)}) custom-call(bf16[960,384]{1,0:T(8,128)(2,1)} %bitcast.11, s32[1,384]{1,0:T(1,128)} %reshape.25.starts, bf16[960,384]{1,0:T(8,128)(2,1)} %bitcast.12, ...), custom_call_target="tpu_custom_call" | custom-call | tf_op jit(solution)/shard_map/layer/pallas_call | solution.py:744
  151.8 11.7 %widen.1 = (f32[960,1280]{1,0:T(8,128)}, f32[480,5120]{1,0:T(8,128)}, f32[480,1600]{1,0:T(8,128)}, f32[480,960]{1,0:T(8,128)}, f32[16,128]{1,0:T(8,128)}, /*index=5*/bf16[960,384]{1,0:T(8,128)(2,1)}, f32[960,384]{1,0:T(8,128)}) custom-call(bf16[2560,16,128]{2,1,0:T(8,128)(2,1)} %get-tuple-element.18.res, bf16[960,384]{1,0:T(8,128)(2,1)} %get-tuple-element.19.mixed_in, ...), custom_call_target="tpu_custom_call" | custom-call | tf_op jit(solution)/shard_map/widen/pallas_call | solution.py:878
  163.4 0.7 slice_bitcast_fusion
  164.1 0.7 dynamic_slice.7
  164.8 0.6 dynamic_slice.6
  (1 shorter events, 0.0 us)

commit v4 on v3

--- a/solution.py
+++ b/solution.py
@@ -57,7 +57,16 @@
 OUT_TICK = 2 * FF_CHUNKS
 ATTN_TICK = OUT_TICK + 1
 LAST_TICK = ATTN_TICK + KEY_VALUE_HEADS
-TICKS = max(2 * FF_CHUNKS + 2 * steps_of(FF_HOPS) - 1, LAST_TICK + 1 + steps_of(QKV_HOPS))
+STEP_TICKS = (
+    (3, 5, 6, 7, 8, 9, 15, 16, 20),
+    (5, 7, 9, 11, 13, 14, 15, 19, 31),
+    (6, 8, 14, 16, 18, 19, 23, 25, 29),
+    (8, 9, 13, 14, 15, 18, 21, 26, 31),
+    (10, 12, 14, 17, 22, 24, 27, 30, 32),
+    (11, 13, 15, 18, 21, 23, 26, 28, 31),
+    (17, 18, 19, 22, 23, 26, 27, 30, 32),
+)
+TICKS = 1 + max(t[-1] for t in STEP_TICKS)
 
 
 def mm(a, b):
@@ -657,44 +666,35 @@
     of_out = ff_travel(5, OUT_BASE, OUT_EXTRA_BASE, OUT_UNITS, OUT_HOPS)
     of_qkv = ff_travel(6, QKV_BASE, QKV_EXTRA_BASE, UNITS, QKV_HOPS)
 
+    groups = [of_ff(g) for g in range(FF_CHUNKS)] + [of_out, of_qkv]
+    chunks = [(g % 2, FF_USED, g * FF_TILES) for g in range(FF_CHUNKS)]
+    chunks += [(1, OUT_USED, OUT_BASE), (0, QKV_USED, QKV_BASE)]
+
+    def take_step(g, k):
+        if k == 0:
+            slot, used, base = chunks[g]
+            pair(g, slot, 0, used, base).wait()
+            add_own(slot, base, used)
+            if g == 6:
+                pair(7, 0, GAIN_TILE, 1, QKV_BASE).wait()
+                at = QKV_BASE + GAIN_TILE
+                work[at] = (work[at].astype(F32) + box[0, core, GAIN_TILE].astype(F32)).astype(BF16)
+        groups[g].step(k)
+
     def travel(tick):
-        for k in range(steps_of(FF_HOPS) - 1, -1, -1):
-            since = tick - 2 - 2 * k
-            turn = lax.rem(since + 64, 4)
-
-            @pl.when((since >= 0) & (since <= 2 * FF_CHUNKS - 2) & ((turn == 0) | (turn == 3)))
-            def _(k=k, since=since):
-                g = lax.div(since, 2)
-                if k == 0:
-                    c = pair(g, lax.rem(g, 2), 0, FF_USED, g * FF_TILES)
-                    c.wait()
-                    add_own(lax.rem(g, 2), g * FF_TILES, FF_USED)
-                of_ff(g).step(k)
-
-        @pl.when(tick > OUT_TICK)
-        def _():
-            for k in range(steps_of(OUT_HOPS)):
-
-                @pl.when(tick == OUT_TICK + 1 + k)
-                def _(k=k):
-                    if k == 0:
-                        pair(5, 1, 0, OUT_USED, OUT_BASE).wait()
-                        add_own(1, OUT_BASE, OUT_USED)
-                    of_out.step(k)
-
-        @pl.when(tick > LAST_TICK)
-        def _():
-            for k in range(steps_of(QKV_HOPS)):
-
-                @pl.when(tick == LAST_TICK + 1 + k)
-                def _(k=k):
-                    if k == 0:
-                        pair(6, 0, 0, QKV_USED, QKV_BASE).wait()
-                        add_own(0, QKV_BASE, QKV_USED)
-                        pair(7, 0, GAIN_TILE, 1, QKV_BASE).wait()
-                        at = QKV_BASE + GAIN_TILE
-                        work[at] = (work[at].astype(F32) + box[0, core, GAIN_TILE].astype(F32)).astype(BF16)
-                    of_qkv.step(k)
+        def some(first, count):
+            @pl.when((tick >= first) & (tick < first + count))
+            def _():
+                if count > 1:
+                    for i in range(0, count, count // 4 if count > 4 else 1):
+                        some(first + i, count // 4 if count > 4 else 1)
+                    return
+                now = [(g, k) for g in range(7) for k, t in enumerate(STEP_TICKS[g]) if t == first]
+                for g, k in sorted(now, key=lambda s: (s[0] if s[0] > 4 else 0, -s[1])):
+                    take_step(g, k)
+
+        for first in range(0, TICKS, 16):
+            some(first, 16)
 
     def tick_body(tick, _):
         @pl.when(tick < OUT_TICK)

time: 166 us -> 156 us (0.940)
  Pallas kernels: 159 us -> 150 us
    pallas_call x1, Pallas kernels: 148 us -> 138 us  [layer(): pl.pallas_call(layer_kernel, out_shape=[shape((D, TOK), BF16), shape((D,...]
where the time goes in v4:
time: 156 us
  Pallas kernels  150 us (96%)
  local copies, waits for them, and re-layouts  4.6 us (3%)
    pallas_call x1, Pallas kernels, layer(): pl.pallas_call(layer_kernel, out_shape=[shape((D, TOK), BF16), shape((D,...  138 us
    pallas_call x1, Pallas kernels, widened(): pl.pallas_call(widen_kernel, out_shape=[shape(s, F32) for s in sizes] + [...  11.7 us

profile of v4, /device:TPU:0, one launch (start us, length us, event | category | flops | bytes accessed | tf_op | source)
XLA Modules:
  0.0 155.6 jit_solution(8270410813150197961)
XLA Ops:
  0.6 1.2 reshape.25.starts
  1.9 0.7 stack.9
  2.6 0.7 stack.10
  3.3 0.7 pad_select_fusion.gains
  4.0 137.9 %layer.1 = (bf16[960,384]{1,0:T(8,128)(2,1)}, f32[960,384]{1,0:T(8,128)}, bf16[2560,16,128]{2,1,0:T(8,128)(2,1)}, bf16[480,5120]{1,0:T(8,128)(2,1)}, bf16[960,1280]{1,0:T(8,128)(2,1)}) custom-call(bf16[960,384]{1,0:T(8,128)(2,1)} %bitcast.11, s32[1,384]{1,0:T(1,128)} %reshape.25.starts, bf16[960,384]{1,0:T(8,128)(2,1)} %bitcast.12, ...), custom_call_target="tpu_custom_call" | custom-call | tf_op jit(solution)/shard_map/layer/pallas_call | solution.py:744
  141.9 11.7 %widen.1 = (f32[960,1280]{1,0:T(8,128)}, f32[480,5120]{1,0:T(8,128)}, f32[480,1600]{1,0:T(8,128)}, f32[480,960]{1,0:T(8,128)}, f32[16,128]{1,0:T(8,128)}, /*index=5*/bf16[960,384]{1,0:T(8,128)(2,1)}, f32[960,384]{1,0:T(8,128)}) custom-call(bf16[2560,16,128]{2,1,0:T(8,128)(2,1)} %get-tuple-element.18.res, bf16[960,384]{1,0:T(8,128)(2,1)} %get-tuple-element.19.mixed_in, ...), custom_call_target="tpu_custom_call" | custom-call | tf_op jit(solution)/shard_map/widen/pallas_call | solution.py:878
  153.6 0.7 slice_bitcast_fusion
  154.3 0.7 dynamic_slice.7
  154.9 0.6 dynamic_slice.6
  (1 shorter events, 0.0 us)

commit v5 on v4

--- a/solution.py
+++ b/solution.py
@@ -58,13 +58,13 @@
 ATTN_TICK = OUT_TICK + 1
 LAST_TICK = ATTN_TICK + KEY_VALUE_HEADS
 STEP_TICKS = (
-    (3, 5, 6, 7, 8, 9, 15, 16, 20),
-    (5, 7, 9, 11, 13, 14, 15, 19, 31),
-    (6, 8, 14, 16, 18, 19, 23, 25, 29),
-    (8, 9, 13, 14, 15, 18, 21, 26, 31),
-    (10, 12, 14, 17, 22, 24, 27, 30, 32),
-    (11, 13, 15, 18, 21, 23, 26, 28, 31),
-    (17, 18, 19, 22, 23, 26, 27, 30, 32),
+    (3, 4, 5, 6, 7, 8, 9, 15, 17),
+    (4, 5, 7, 8, 9, 11, 14, 21, 32),
+    (6, 7, 9, 12, 15, 16, 22, 27, 31),
+    (8, 10, 14, 17, 19, 20, 24, 29, 33),
+    (10, 13, 15, 19, 23, 25, 28, 31, 34),
+    (13, 15, 19, 21, 24, 27, 30, 31, 34),
+    (17, 19, 21, 23, 24, 27, 29, 30, 33),
 )
 TICKS = 1 + max(t[-1] for t in STEP_TICKS)
 

time: 156 us -> 153 us (0.981)
  Pallas kernels: 150 us -> 147 us
    pallas_call x1, Pallas kernels: 138 us -> 135 us  [layer(): pl.pallas_call(layer_kernel, out_shape=[shape((D, TOK), BF16), shape((D,...]
where the time goes in v5:
time: 153 us
  Pallas kernels  147 us (96%)
  local copies, waits for them, and re-layouts  4.6 us (3%)
    pallas_call x1, Pallas kernels, layer(): pl.pallas_call(layer_kernel, out_shape=[shape((D, TOK), BF16), shape((D,...  135 us
    pallas_call x1, Pallas kernels, widened(): pl.pallas_call(widen_kernel, out_shape=[shape(s, F32) for s in sizes] + [...  11.7 us

profile of v5, /device:TPU:0, one launch (start us, length us, event | category | flops | bytes accessed | tf_op | source)
XLA Modules:
  0.0 152.6 jit_solution(12802802098431428719)
XLA Ops:
  0.6 1.2 reshape.25.starts
  1.9 0.7 stack.9
  2.6 0.7 stack.10
  3.3 0.7 pad_select_fusion.gains
  4.0 135.0 %layer.1 = (bf16[960,384]{1,0:T(8,128)(2,1)}, f32[960,384]{1,0:T(8,128)}, bf16[2560,16,128]{2,1,0:T(8,128)(2,1)}, bf16[480,5120]{1,0:T(8,128)(2,1)}, bf16[960,1280]{1,0:T(8,128)(2,1)}) custom-call(bf16[960,384]{1,0:T(8,128)(2,1)} %bitcast.11, s32[1,384]{1,0:T(1,128)} %reshape.25.starts, bf16[960,384]{1,0:T(8,128)(2,1)} %bitcast.12, ...), custom_call_target="tpu_custom_call" | custom-call | tf_op jit(solution)/shard_map/layer/pallas_call | solution.py:744
  139.0 11.7 %widen.1 = (f32[960,1280]{1,0:T(8,128)}, f32[480,5120]{1,0:T(8,128)}, f32[480,1600]{1,0:T(8,128)}, f32[480,960]{1,0:T(8,128)}, f32[16,128]{1,0:T(8,128)}, /*index=5*/bf16[960,384]{1,0:T(8,128)(2,1)}, f32[960,384]{1,0:T(8,128)}) custom-call(bf16[2560,16,128]{2,1,0:T(8,128)(2,1)} %get-tuple-element.18.res, bf16[960,384]{1,0:T(8,128)(2,1)} %get-tuple-element.19.mixed_in, ...), custom_call_target="tpu_custom_call" | custom-call | tf_op jit(solution)/shard_map/widen/pallas_call | solution.py:878
  150.7 0.7 slice_bitcast_fusion
  151.3 0.7 dynamic_slice.7
  152.0 0.6 dynamic_slice.6
  (1 shorter events, 0.0 us)
